TPU v7x, 256 devices: a whole 4x4x8 slice. The times are simulated.
256 devices in a mesh: group: 32 (over y, z), tensor: 8 (over x, core).
Axes of the slice: x: 4, y: 4, z: 8, core: 2. Of those that a mesh axis runs over, the one named last changes fastest.
Arguments:
- stretch_query_rows: bfloat16 [49152, 8192], P('group', 'tensor'), may hold values from -7 to 7
- earlier_token_cache: bfloat16 [1024, 192, 2, 1024], P('group', None, None, 'tensor'), may hold values from -6 to 6
- stretch_cache: bfloat16 [1024, 48, 2, 1024], P('group', None, None, 'tensor'), may hold values from -6 to 6
- stretch_position: int32 [1024], P('group'), may hold values from 16 to 192, as said below
- owning_decode_group: int32 [1024], P('group'), may hold values from 0 to 31, as said below
- decode_query_rows: bfloat16 [2048, 8192], P('group', 'tensor'), may hold values from -7 to 7
- decode_input_rows: bfloat16 [2048, 8192], P('group', 'tensor'), may hold values from -6 to 6
- decode_base_projection: bfloat16 [2048, 2, 1024], P('group', None, 'tensor'), may hold values from -6 to 6
- row_adapter_index: int32 [2048], P('group'), may hold values from 0 to 7
- adapter_down_weight: bfloat16 [8192, 256], P('tensor'), may hold values from -0.0625 to 0.0625
- adapter_up_weight: bfloat16 [256, 1024], P(None, 'tensor'), may hold values from -1.5 to 1.5
- group_page_store: bfloat16 [3072, 16, 2, 1024], P('group', None, None, 'tensor'), may hold values from -6 to 6
- row_page_index: int32 [2048, 15], P('group'), may hold values from 0 to 287, as said below
- cached_token_length: int32 [2048], P('group'), may hold values from 1 to 240
Outputs:
- prefill_out: bfloat16 [49152, 8192], P('group', 'tensor')
- decode_out: bfloat16 [2048, 8192], P('group', 'tensor')
Inputs may be any that keep to these rules, and one draw needn't show every extreme that they name: `owning_decode_group`: at most 2 prompts of one prefill group name the same decode group, and some decode group is named by exactly 2 prompts of every group. `stretch_position`: multiples of 16. `row_page_index`: an entry e >= 96 names landing page e - 96 of the row's group, and only pages that hold a prompt's tokens are named. Entries at and beyond position (cached_token_length[r] - 1) // 16 + 1 are not read.
All inputs are finite; a program needn't handle non-finite values.
Results may differ from a plain program's by a relative error of at most 0.02.
Values may be sent and summed in bfloat16 or wider, within the bound.
No kernel may reach another device: no remote copies, remote signals or barrier semaphores. Data moves between devices by JAX's collectives and lax.ppermute only.
A program may use at most 128 MiB of HBM per device.

v0:
```python
import jax
import jax.numpy as jnp
from jax import lax
from jax.sharding import PartitionSpec as P

HEAD_SIZE = 128
ADAPTER_RANK = 16
ADAPTER_COUNT = 8
PAGE = 16
PROMPTS_GRP = 32


ADAPTER_SCALE = 2.0


def prompt_slots(owning_decode_group):
    group_sorted = owning_decode_group.reshape(-1, PROMPTS_GRP)
    same_dest = group_sorted[:, :, None] == group_sorted[:, None, :]
    order_index = jnp.arange(PROMPTS_GRP, dtype=jnp.int32)
    earlier = order_index[None, :] < order_index[:, None]
    return jnp.sum((same_dest & earlier[None]).astype(jnp.int32), axis=2).reshape(-1)


def prefill_part(stretch_query_rows, earlier_token_cache, stretch_cache, stretch_position):
    prompt_count, prefix_len = (earlier_token_cache.shape[0], earlier_token_cache.shape[1])
    stretch_len = stretch_cache.shape[1]
    key_value_features = earlier_token_cache.shape[-1]
    kv_heads = key_value_features // HEAD_SIZE
    per_head = stretch_query_rows.shape[1] // key_value_features
    query_block = stretch_query_rows.reshape(
        prompt_count, stretch_len, kv_heads, per_head, HEAD_SIZE
    )
    earlier_keys = earlier_token_cache[:, :, 0].reshape(
        prompt_count, prefix_len, kv_heads, HEAD_SIZE
    )
    earlier_values = earlier_token_cache[:, :, 1].reshape(
        prompt_count, prefix_len, kv_heads, HEAD_SIZE
    )
    stretch_keys = stretch_cache[:, :, 0].reshape(prompt_count, stretch_len, kv_heads, HEAD_SIZE)
    stretch_values = stretch_cache[:, :, 1].reshape(prompt_count, stretch_len, kv_heads, HEAD_SIZE)
    score_scale = HEAD_SIZE ** (-0.5)
    prefix_scores = (
        jnp.einsum(
            "pqgmd,ptgd->pgmqt", query_block, earlier_keys, preferred_element_type=jnp.float32
        )
        * score_scale
    )
    fresh_scores = (
        jnp.einsum(
            "pqgmd,pjgd->pgmqj", query_block, stretch_keys, preferred_element_type=jnp.float32
        )
        * score_scale
    )
    seen = jnp.arange(prefix_len, dtype=jnp.int32)[None, :] < stretch_position[:, None]
    prefix_scores = jnp.where(seen[:, None, None, None, :], prefix_scores, -jnp.inf)
    stretch_index = jnp.arange(stretch_len, dtype=jnp.int32)
    causal = stretch_index[None, :] <= stretch_index[:, None]
    fresh_scores = jnp.where(causal[None, None, None], fresh_scores, -jnp.inf)
    row_maximum = jnp.maximum(prefix_scores.max(-1), fresh_scores.max(-1))
    prefix_exp = jnp.exp(prefix_scores - row_maximum[..., None])
    fresh_exp = jnp.exp(fresh_scores - row_maximum[..., None])
    row_total = prefix_exp.sum(-1) + fresh_exp.sum(-1)
    prefix_weights = (prefix_exp / row_total[..., None]).astype(jnp.bfloat16)
    fresh_weights = (fresh_exp / row_total[..., None]).astype(jnp.bfloat16)
    attended = jnp.einsum(
        "pgmqt,ptgd->pqgmd", prefix_weights, earlier_values, preferred_element_type=jnp.float32
    )
    attended = attended + jnp.einsum(
        "pgmqj,pjgd->pqgmd", fresh_weights, stretch_values, preferred_element_type=jnp.float32
    )
    return attended.reshape(prompt_count * stretch_len, -1).astype(jnp.bfloat16)


def adapter_correction(
    decode_input_rows,
    row_adapter_index,
    adapter_down_weight,
    adapter_up_weight,
    decode_base_projection,
):
    row_count = decode_input_rows.shape[0]
    down_projected_rows = jnp.dot(
        decode_input_rows, adapter_down_weight, preferred_element_type=jnp.float32
    ).reshape(row_count, ADAPTER_COUNT, 2 * ADAPTER_RANK)
    choose = row_adapter_index[:, None] == jnp.arange(ADAPTER_COUNT, dtype=jnp.int32)[None, :]
    picked = jnp.sum(jnp.where(choose[:, :, None], down_projected_rows, 0.0), axis=1)
    summed = lax.psum(picked, "tensor")
    middle = summed.astype(jnp.bfloat16)
    broadcast_rows = jnp.where(
        choose[:, :, None], middle[:, None, :], jnp.zeros((), jnp.bfloat16)
    ).reshape(row_count, ADAPTER_COUNT, 2, ADAPTER_RANK)
    key_value_features = adapter_up_weight.shape[1]
    up_weight_rows = adapter_up_weight.reshape(ADAPTER_COUNT, 2, ADAPTER_RANK, key_value_features)
    adapter_delta = jnp.einsum(
        "bsqo,sqon->bqn", broadcast_rows, up_weight_rows, preferred_element_type=jnp.float32
    )
    return (decode_base_projection.astype(jnp.float32) + ADAPTER_SCALE * adapter_delta).astype(
        jnp.bfloat16
    )


def select_pages(table, first, count):
    wanted = first + jnp.arange(count, dtype=jnp.int32)
    return (table[:, :, None] == wanted[None, None, :]).astype(jnp.bfloat16)


def decode_part(
    decode_query_rows,
    group_page_store,
    landing,
    row_page_index,
    cached_token_length,
    incoming_key_value,
):
    row_count = decode_query_rows.shape[0]
    key_value_features = group_page_store.shape[-1]
    kv_heads = key_value_features // HEAD_SIZE
    per_head = decode_query_rows.shape[1] // key_value_features
    pool_count = group_page_store.shape[0]
    page_feature = PAGE * 2 * key_value_features
    pool_flat = group_page_store.reshape(pool_count, page_feature)
    landing_flat = landing.reshape(-1, page_feature)
    pool_pick = select_pages(row_page_index, 0, pool_count)
    landing_pick = select_pages(row_page_index, pool_count, landing_flat.shape[0])
    collected_sum = jnp.einsum(
        "rpe,ef->rpf", pool_pick, pool_flat, preferred_element_type=jnp.float32
    )
    collected_sum = collected_sum + jnp.einsum(
        "rpe,ef->rpf", landing_pick, landing_flat, preferred_element_type=jnp.float32
    )
    table_width = row_page_index.shape[1]
    collected_pages = collected_sum.astype(jnp.bfloat16).reshape(
        row_count, table_width, PAGE, 2, key_value_features
    )
    cache_extent = table_width * PAGE
    paged_keys = collected_pages[:, :, :, 0].reshape(row_count, cache_extent, kv_heads, HEAD_SIZE)
    paged_values = collected_pages[:, :, :, 1].reshape(row_count, cache_extent, kv_heads, HEAD_SIZE)
    query_block = decode_query_rows.reshape(row_count, kv_heads, per_head, HEAD_SIZE)
    own_keys = incoming_key_value[:, 0].reshape(row_count, kv_heads, HEAD_SIZE)
    own_values = incoming_key_value[:, 1].reshape(row_count, kv_heads, HEAD_SIZE)
    score_scale = HEAD_SIZE ** (-0.5)
    cache_scores = (
        jnp.einsum("rgmd,rtgd->rgmt", query_block, paged_keys, preferred_element_type=jnp.float32)
        * score_scale
    )
    own_scores = (
        jnp.einsum("rgmd,rgd->rgm", query_block, own_keys, preferred_element_type=jnp.float32)
        * score_scale
    )
    visible = jnp.arange(cache_extent, dtype=jnp.int32)[None, :] < cached_token_length[:, None]
    cache_scores = jnp.where(visible[:, None, None, :], cache_scores, -jnp.inf)
    row_maximum = jnp.maximum(cache_scores.max(-1), own_scores)
    cache_exp = jnp.exp(cache_scores - row_maximum[..., None])
    own_exp = jnp.exp(own_scores - row_maximum)
    row_total = cache_exp.sum(-1) + own_exp
    cache_weights = (cache_exp / row_total[..., None]).astype(jnp.bfloat16)
    own_weights = (own_exp / row_total).astype(jnp.bfloat16)
    attended = jnp.einsum(
        "rgmt,rtgd->rgmd", cache_weights, paged_values, preferred_element_type=jnp.float32
    )
    attended = (
        attended
        + own_weights.astype(jnp.float32)[..., None] * own_values.astype(jnp.float32)[:, :, None, :]
    )
    return attended.reshape(row_count, -1).astype(jnp.bfloat16)


def body(
    stretch_query_rows,
    earlier_token_cache,
    stretch_cache,
    stretch_position,
    owning_decode_group,
    decode_query_rows,
    decode_input_rows,
    decode_base_projection,
    row_adapter_index,
    adapter_down_weight,
    adapter_up_weight,
    group_page_store,
    row_page_index,
    cached_token_length,
):
    prompt_count = stretch_cache.shape[0]
    group_count = lax.axis_size("group")
    capacity = max(2, (prompt_count + group_count - 1) // group_count)
    slot_count = group_count * capacity
    slot_ranks = prompt_slots(owning_decode_group)
    stretch_flat = stretch_cache.reshape(prompt_count, -1)
    slot_index = jnp.arange(slot_count, dtype=jnp.int32)
    member = lax.axis_index("group")
    piece_cache = lax.all_gather(stretch_flat, "group", axis=0, tiled=True)
    piece_dest = lax.all_gather(owning_decode_group, "group", axis=0, tiled=True)
    piece_slot = lax.all_gather(slot_ranks, "group", axis=0, tiled=True)
    sources = jnp.arange(piece_dest.shape[0], dtype=jnp.int32) // prompt_count
    target_slot = jnp.where(piece_dest == member, sources * capacity + piece_slot, slot_count)
    placement = (slot_index[:, None] == target_slot[None, :]).astype(jnp.bfloat16)
    landed = jnp.dot(placement, piece_cache, preferred_element_type=jnp.float32)
    landing = landed.astype(jnp.bfloat16).reshape((slot_count,) + stretch_cache.shape[1:])
    incoming_key_value = adapter_correction(
        decode_input_rows,
        row_adapter_index,
        adapter_down_weight,
        adapter_up_weight,
        decode_base_projection,
    )
    prefill_out = prefill_part(
        stretch_query_rows, earlier_token_cache, stretch_cache, stretch_position
    )
    decode_out = decode_part(
        decode_query_rows,
        group_page_store,
        landing,
        row_page_index,
        cached_token_length,
        incoming_key_value,
    )
    return (prefill_out, decode_out)


def solution(mesh):
    placed = (
        P("group", "tensor"),
        P("group", None, None, "tensor"),
        P("group", None, None, "tensor"),
        P("group"),
        P("group"),
        P("group", "tensor"),
        P("group", "tensor"),
        P("group", None, "tensor"),
        P("group"),
        P("tensor", None),
        P(None, "tensor"),
        P("group", None, None, "tensor"),
        P("group", None),
        P("group"),
    )
    return jax.shard_map(
        body,
        mesh=mesh,
        in_specs=placed,
        out_specs=(P("group", "tensor"), P("group", "tensor")),
        check_vma=False,
    )
```

profile of v0, /device:TPU:2, one launch (start us, length us, event | category | flops | bytes accessed | tf_op | source)
XLA Modules:
  0.0 264.5 jit_solution(17141904647243647683)
XLA Ops:
  7.2 3.2 %reshape.318 = bf16[32,12288]{1,0:T(8,128)(2,1)} reshape(bf16[32,48,2,128]{3,2,1,0:T(2,128)(2,1)} %param.16) | data formatting | bytes 1572864 | tf_op jit(solution)/shard_map/reshape | solution.py:189
  10.5 2.4 reshape.341
  13.0 0.9 copy.69
  13.9 2.7 %copy.67 = bf16[192,8,8,128]{3,2,1,0:T(8,128)(2,1)S(1)} copy(bf16[192,8,8,128]{3,1,2,0:T(8,128)(2,1)} %bitcast.148) | data formatting | bytes 6291456
  16.7 1.1 fusion.60
  17.8 3.5 %fusion.6 = (f32[32,8,48]{2,1,0:T(8,128)S(1)}, f32[32,48,48,8]{2,1,3,0:T(8,128)S(1)}) fusion(pred[48,48]{0,1:T(8,128)(4,1)S(1)} %iota_compare_fusion.6, bf16[32,48,8,128]{3,2,1,0:T(8,128)(2,1)S(1)} %bitcast.144, bf16[32,48,1,128]{3,2,1,0:T(2,128)(2,1)S(1)} %get-tuple-element.9), kind=kOutput, calls=%fused_computation.16 | convolution fusion | flops 152752128 | bytes 5949696 | tf_op jit(solution)/shard_map/pqgmd,pjgd->pgmqj/dot_general | solution.py:49
  21.4 5.6 %fusion.59 = (bf16[32,192,1,128]{3,2,1,0:T(2,128)(2,1)S(1)}, bf16[32,192,1,128]{3,2,1,0:T(2,128)(2,1)}) fusion(bf16[32,192,2,128]{3,2,1,0:T(2,128)(2,1)S(1)} %copy-done.2), kind=kLoop, calls=%fused_computation.97 | loop fusion | bytes 6291456 | tf_op jit(solution)/shard_map/slice | solution.py:36
  27.0 8.3 %bitcast_reduce_fusion = (f32[32,8,48]{2,1,0:T(8,128)S(1)}, f32[32,192,48,8]{1,2,3,0:T(8,128)}) fusion(pred[32,192]{1,0:T(8,128)(4,1)S(1)} %iota_compare_fusion.5, bf16[32,48,8,128]{3,2,1,0:T(8,128)(2,1)S(1)} %bitcast.145, bf16[32,192,1,128]{3,2,1,0:T(2,128)(2,1)} %get-tuple-element.7), kind=kOutput, calls=%fused_computation.3 | convolution fusion | flops 611045376 | bytes 14211072 | tf_op jit(solution)/shard_map/pqgmd,ptgd->pgmqt/dot_general | solution.py:43
  35.3 2.2 fusion.5
  37.5 8.7 %fusion.1 = f32[32,8,48]{2,1,0:T(8,128)S(1)} fusion(f32[32,192,48,8]{1,2,3,0:T(8,128)} %get-tuple-element.15, f32[32,8,48]{2,1,0:T(8,128)S(1)} %max.13, pred[32,192]{1,0:T(8,128)(4,1)S(1)} %iota_compare_fusion.5), kind=kLoop, calls=%fused_computation.7 | loop fusion | flops 9424896 | bytes 9541632 | tf_op jit(solution)/shard_map/reduce_sum | solution.py:62
  46.3 6.7 %fusion.2 = f32[32,8,48,128]{3,2,1,0:T(8,128)} fusion(f32[32,192,48,8]{1,2,3,0:T(8,128)S(1)} %copy-done.3, f32[32,8,48]{2,1,0:T(8,128)S(1)} %add.45, f32[32,8,48]{2,1,0:T(8,128)S(1)} %max.13, pred[32,192]{1,0:T(8,128)(4,1)S(1)} %iota_compare_fusion.5, bf16[32,192,1,128]{3,2,1,0:T(2,128)(2,1)S(1)} %get-tuple-element.6), kind=kOutput, calls=%fused_computation.9 | convolution fusion | flops 615776256 | bytes 17405952 | tf_op jit(solution)/shard_map/pgmqt,ptgd->pqgmd/dot_general | solution.py:65
  53.0 4.3 %fusion.7 = bf16[32,48,1,8,128]{4,1,3,0,2:T(8,128)(2,1)S(1)} fusion(f32[32,8,48,128]{3,2,1,0:T(8,128)} %fusion.2, f32[32,8,48]{2,1,0:T(8,128)S(1)} %add.45, f32[32,48,48,8]{2,1,3,0:T(8,128)S(1)} %get-tuple-element.17, f32[32,8,48]{2,1,0:T(8,128)S(1)} %max.13, pred[48,48]{0,1:T(8,128)(4,1)S(1)} %iota_compare_fusion.6, ...), kind=kOutput, calls=%fused_computation.17 | convolution fusion | flops 157089792 | bytes 12290304 | tf_op jit(solution)/shard_map/pgmqj,pjgd->pqgmd/dot_general | solution.py:68
  57.4 0.8 copy.48
  58.2 2.5 copy.98
  60.7 0.6 dynamic-slice
  62.0 0.2 dynamic-update-slice
  62.4 0.2 dynamic-update-slice.1
  62.7 24.1 %all-reduce.2 = (s32[1024]{0:T(1024)S(1)}, s32[1024]{0:T(1024)S(1)}) all-reduce(s32[1024]{0:T(1024)S(1)} %dynamic-update-slice.1, s32[1024]{0:T(1024)S(1)} %dynamic-update-slice), channel_id=1, replica_groups=mesh['group'=32,'tensor'=8] {'group'}, use_global_device_ids=true, to_apply=%add.1 | all-reduce | flops 2048 | bytes 16384
  86.8 0.3 fusion.62
  87.2 21.8 %psum.7 = bf16[64,32]{0,1:T(8,128)(2,1)S(1)} all-reduce(f32[64,32]{0,1:T(8,128)S(1)} %select_reduce_fusion), channel_id=1, replica_groups=mesh['group'=32,'tensor'=8] {'tensor'}, use_global_device_ids=true, to_apply=%region_7.8 | all-reduce | flops 2048 | bytes 12288 | tf_op jit(solution)/shard_map/psum | solution.py:87
  109.6 7.7 %fusion.30 = f32[64,15,4096]{2,0,1:T(8,128)} fusion(bf16[96,4096,1]{1,0,2:T(8,128)(2,1)S(1)} %reshape.341, s32[64,15]{0,1:T(8,128)S(1)} %copy-done.6), kind=kOutput, calls=%fused_computation.47 | convolution fusion | flops 755066880 | bytes 16518912 | tf_op jit(solution)/shard_map/rpe,ef->rpf/dot_general | solution.py:125
  117.3 80.3 %all-gather.2.cloned.1.call-done = bf16[1024,12288]{1,0:T(8,128)(2,1)} async-done(((bf16[32,12288]{1,0:T(8,128)(2,1)}), bf16[1024,12288]{1,0:T(8,128)(2,1)}) %all-gather.2.cloned.1.call-update) | async-done | bytes 25165840 | tf_op jit(solution)/shard_map/all_gather | solution.py:192
  197.5 13.8 %convolution_convert_fusion = bf16[64,12288]{1,0:T(8,128)(2,1)} fusion(bf16[1024,12288]{1,0:T(8,128)(2,1)} %all-gather.2.cloned.1.call-done, s32[1024]{0:T(1024)S(1)} %fusion.49), kind=kOutput, calls=%fused_computation.1 | convolution fusion | flops 1611464704 | bytes 26742784 | tf_op jit(solution)/shard_map/dot_general | solution.py:198
  211.4 2.7 %reshape.342 = bf16[192,4096,1]{1,0,2:T(8,128)(2,1)S(1)} reshape(bf16[64,12288]{1,0:T(8,128)(2,1)} %convolution_convert_fusion) | data formatting | bytes 3145728 | tf_op jit(solution)/shard_map/reshape;reshape | solution.py:122
  214.1 8.6 %add_convert_fusion = bf16[64,15,4096]{2,0,1:T(8,128)(2,1)} fusion(f32[64,15,4096]{2,0,1:T(8,128)} %fusion.30, bf16[192,4096,1]{1,0,2:T(8,128)(2,1)S(1)} %reshape.342, s32[192]{0:T(256)S(1)} %iota_add_fusion, s32[64,15]{0,1:T(8,128)S(1)} %copy-done.6), kind=kOutput, calls=%fused_computation | convolution fusion | flops 1517998080 | bytes 25170432 | tf_op jit(solution)/shard_map/rpe,ef->rpf/dot_general | solution.py:128
  222.7 13.6 %reshape.319 = bf16[64,15,16,2,128]{4,3,2,0,1:T(2,128)(2,1)} reshape(bf16[64,15,4096]{2,0,1:T(8,128)(2,1)} %add_convert_fusion) | data formatting | bytes 15728640 | tf_op jit(solution)/shard_map/reshape | solution.py:132
  236.3 15.9 %fusion.58 = (bf16[64,15,16,1,128]{4,3,2,0,1:T(2,128)(2,1)S(1)}, bf16[64,15,16,1,128]{4,3,2,0,1:T(2,128)(2,1)S(1)}) fusion(bf16[64,15,16,2,128]{4,3,2,0,1:T(2,128)(2,1)} %reshape.319), kind=kLoop, calls=%fused_computation.96 | loop fusion | bytes 15728640 | tf_op jit(solution)/shard_map/slice | solution.py:136
  252.2 0.5 copy.49
  252.7 2.2 fusion.61
  255.2 0.5 copy.53
  255.7 1.2 fusion.22
  256.9 0.7 copy.99
  (48 shorter events, 1.2 us)
Async XLA Ops:
  7.2 79.6 %copy-start = (bf16[1024,256]{1,0:T(8,128)(2,1)S(1)}, bf16[1024,256]{1,0:T(8,128)(2,1)}, u32[]{:S(2)}) copy-start(bf16[1024,256]{1,0:T(8,128)(2,1)} %param.23) | copy-start | bytes 1572868
  7.2 9.5 %copy-start.4 = (bf16[32,48,2,128]{3,2,1,0:T(2,128)(2,1)S(1)}, bf16[32,48,2,128]{3,2,1,0:T(2,128)(2,1)}, u32[]{:S(2)}) copy-start(bf16[32,48,2,128]{3,2,1,0:T(2,128)(2,1)} %param.16) | copy-start | bytes 2359300
  7.2 9.4 %copy-start.7 = (s32[32]{0:T(128)S(1)}, s32[32]{0:T(128)}, u32[]{:S(2)}) copy-start(s32[32]{0:T(128)} %param.17) | copy-start | bytes 388
  7.2 190.3 %all-gather.2.cloned.1.call-start = ((), (), s32[]{:S(2)}) async-start(), calls=%async_computation | async-start | bytes 25952256 | tf_op jit(solution)/shard_map/all_gather | solution.py:192
  16.7 4.7 %copy-start.2 = (bf16[32,192,2,128]{3,2,1,0:T(2,128)(2,1)S(1)}, bf16[32,192,2,128]{3,2,1,0:T(2,128)(2,1)}, u32[]{:S(2)}) copy-start(bf16[32,192,2,128]{3,2,1,0:T(2,128)(2,1)} %param.15) | copy-start | bytes 9437188
  37.5 8.8 %copy-start.3 = (f32[32,192,48,8]{1,2,3,0:T(8,128)S(1)}, f32[32,192,48,8]{1,2,3,0:T(8,128)}, u32[]{:S(2)}) copy-start(f32[32,192,48,8]{1,2,3,0:T(8,128)} %get-tuple-element.15) | copy-start | bytes 28311556
  57.3 3.4 %copy-start.13 = (u32[256]{0:T(256)S(1)}, u32[256]{0:T(256)}, u32[]{:S(2)}) copy-start(u32[256]{0:T(256)} %constant.46) | copy-start | bytes 3076
  57.3 4.6 %copy-start.11 = (s32[32]{0:T(128)S(1)}, s32[32]{0:T(128)}, u32[]{:S(2)}) copy-start(s32[32]{0:T(128)} %param.18) | copy-start | bytes 388
  57.3 29.5 %copy-start.12 = (s32[64]{0:T(128)S(1)}, s32[64]{0:T(128)}, u32[]{:S(2)}) copy-start(s32[64]{0:T(128)} %param.22) | copy-start | bytes 772
  57.4 29.5 %copy-start.5 = (bf16[64,1024]{1,0:T(8,128)(2,1)S(1)}, bf16[64,1024]{1,0:T(8,128)(2,1)}, u32[]{:S(2)}) copy-start(bf16[64,1024]{1,0:T(8,128)(2,1)} %param.20) | copy-start | bytes 393220
  57.4 51.7 %copy-start.8 = (s32[64]{0:T(128)S(1)}, s32[64]{0:T(128)}, u32[]{:S(2)}) copy-start(s32[64]{0:T(128)} %param.27) | copy-start | bytes 772
  57.4 51.7 %copy-start.9 = (bf16[256,128]{1,0:T(8,128)(2,1)S(1)}, bf16[256,128]{1,0:T(8,128)(2,1)}, u32[]{:S(2)}) copy-start(bf16[256,128]{1,0:T(8,128)(2,1)} %param.24) | copy-start | bytes 196612
  57.4 51.7 %copy-start.10 = (bf16[64,2,128]{2,1,0:T(2,128)(2,1)S(1)}, bf16[64,2,128]{2,1,0:T(2,128)(2,1)}, u32[]{:S(2)}) copy-start(bf16[64,2,128]{2,1,0:T(2,128)(2,1)} %param.21) | copy-start | bytes 98308
  57.4 52.2 %copy-start.6 = (s32[64,15]{0,1:T(8,128)S(1)}, s32[64,15]{0,1:T(8,128)}, u32[]{:S(2)}) copy-start(s32[64,15]{0,1:T(8,128)} %param.26) | copy-start | bytes 11524
  255.2 2.4 copy-start.1
Sparse Core Ops, SparseCore 0:
  10.6 186.8 all-gather.1
where the time goes:
time: 266 us; the launch traced here: 264 us
  waiting for transfers between devices  80.3 us (30%)
  matrix products  57.1 us (21%)
  local copies, waits for them, and re-layouts  54.4 us (20%)
  blocking collectives  46 us (17%)
  between operations  15.1 us (6%)
  other arithmetic  11.6 us (4%)
    all_gather x1, waiting for transfers between devices, body(): piece_cache = lax.all_gather(stretch_flat, 'group', axis=0, tiled=True)  80.3 us
    unnamed x1, blocking collectives  24.1 us
    psum x1, blocking collectives, adapter_correction(): summed = lax.psum(picked, 'tensor')  21.8 us
    slice x2, local copies, waits for them, and re-layouts, decode_part(): collected_pages[:, :, :, 0]  16.4 us
    dot_general x1, matrix products, body(): landed = jnp.dot(placement, piece_cache, preferred_element_type=jnp.float32)  13.8 us
    reshape x1, local copies, waits for them, and re-layouts, decode_part(): collected_sum.astype(jnp.bfloat16)  13.6 us
    reduce_sum x2, other arithmetic, prefill_part(): row_total = prefix_exp.sum(-1) + fresh_exp.sum(-1)  10.9 us
    dot_general x1, matrix products, decode_part(): jnp.einsum('rpe,ef->rpf', landing_pick, landing_flat, preferred_element_t...  8.61 us
  transfers between devices with their start and end apart: 1, of which 1 were waited for; matrix products, arithmetic and copies ran while one was open for 23% of the time, Pallas kernels for 0%

commit v1 on v0

v1 whole, which is shorter than its diff:
```python
import functools

import jax
import jax.numpy as jnp
from jax import lax
from jax.experimental import pallas as pl
from jax.experimental.pallas import tpu as pltpu
from jax.sharding import PartitionSpec as P

HEAD_SIZE = 128
ADAPTER_RANK = 16
ADAPTER_COUNT = 8
PAGE = 16
CAP = 2
ADAPTER_SCALE = 2.0
SCORE_SCALE = HEAD_SIZE ** (-0.5) * 1.4426950408889634
MASKED = -1e30
VMEM_BYTES = 24 * 1024 * 1024
PACK_BYTES = 56 * 1024 * 1024
PROMPT_BLOCK = 8
HEAD_BLOCK = 4
LANDING_TOKENS = 768

CONTRACT_LAST = (((1,), (1,)), ((), ()))


def in_vmem():
    return pl.BlockSpec(memory_space=pltpu.VMEM)


def in_smem():
    return pl.BlockSpec(memory_space=pltpu.SMEM)


def params(limit=VMEM_BYTES):
    return pltpu.CompilerParams(vmem_limit_bytes=limit)


def cost(flops, moved, exps=0):
    return pl.CostEstimate(flops=flops, bytes_accessed=moved, transcendentals=exps)


def pack_kernel(
    owner_hbm, kv_hbm, out_hbm, owner_ref, kv_ref, split_ref, stage_ref, zero_ref, count_ref, slot_ref,
    owner_sem, kv_sem, out_sem,
):
    prompts, rows, _ = kv_ref.shape
    tokens = rows // 2
    groups, cap = out_hbm.shape[:2]
    parts = kv_sem.shape[0]
    span = prompts // parts
    owner_copy = pltpu.make_async_copy(owner_hbm, owner_ref, owner_sem)
    owner_copy.start()
    kv_copies = [
        pltpu.make_async_copy(
            kv_hbm.at[pl.ds(c * span, span)], kv_ref.at[pl.ds(c * span, span)], kv_sem.at[c]
        )
        for c in range(parts)
    ]
    for copy in kv_copies:
        copy.start()
    zero_ref[...] = jnp.zeros_like(zero_ref)
    for d in range(groups):
        count_ref[d] = 0
    owner_copy.wait()
    for p in range(prompts):
        dest = owner_ref[p]
        rank = count_ref[dest]
        count_ref[dest] = rank + 1
        slot_ref[p] = jnp.minimum(rank, cap - 1)
    for c in range(parts):
        kv_copies[c].wait()
        block = slice(c * span, (c + 1) * span)
        split_ref[block] = kv_ref[block].astype(jnp.float32)
        for p in range(c * span, (c + 1) * span):
            for j in range(2):
                part = split_ref[p, pl.ds(j, tokens, stride=2), :]
                stage_ref[p, j * tokens : (j + 1) * tokens] = part.astype(jnp.bfloat16)
        for p in range(c * span, (c + 1) * span):
            pltpu.make_async_copy(
                stage_ref.at[p], out_hbm.at[owner_ref[p], slot_ref[p]], out_sem
            ).start()
    for d in range(groups):
        for slot in range(cap):

            @pl.when(count_ref[d] <= slot)
            def _():
                pltpu.make_async_copy(zero_ref, out_hbm.at[d, slot], out_sem).start()

    pltpu.make_async_copy(out_hbm, out_hbm, out_sem).wait()


def pack(owner, stretch, groups):
    prompts, rows, _ = stretch.shape
    parts = 4
    return pl.pallas_call(
        pack_kernel,
        out_shape=jax.ShapeDtypeStruct((groups, CAP, rows, HEAD_SIZE), jnp.bfloat16),
        in_specs=[pl.BlockSpec(memory_space=pl.ANY)] * 2,
        out_specs=pl.BlockSpec(memory_space=pl.ANY),
        scratch_shapes=[
            pltpu.SMEM((prompts,), jnp.int32),
            pltpu.VMEM(stretch.shape, jnp.bfloat16),
            pltpu.VMEM(stretch.shape, jnp.float32),
            pltpu.VMEM(stretch.shape, jnp.bfloat16),
            pltpu.VMEM((rows, HEAD_SIZE), jnp.bfloat16),
            pltpu.SMEM((groups,), jnp.int32),
            pltpu.SMEM((prompts,), jnp.int32),
            pltpu.SemaphoreType.DMA,
            pltpu.SemaphoreType.DMA((parts,)),
            pltpu.SemaphoreType.DMA,
        ],
        compiler_params=params(PACK_BYTES),
        cost_estimate=cost(0, stretch.size * 2 + groups * CAP * rows * HEAD_SIZE * 2),
        name="pack",
    )(owner, stretch)


def prefill_kernel(pos_ref, query_ref, earlier_ref, stretch_ref, out_ref, split_ref):
    block, earlier_rows, _ = earlier_ref.shape
    fresh_rows = stretch_ref.shape[1]
    prefix, fresh = earlier_rows // 2, fresh_rows // 2
    keys = split_ref.shape[1] // 2
    heads = query_ref.shape[1] // HEAD_SIZE
    step = pl.program_id(0)

    @pl.when(step == 0)
    def _():
        split_ref[...] = jnp.zeros_like(split_ref)

    column = lax.broadcasted_iota(jnp.int32, (fresh, keys), 1)
    row = lax.broadcasted_iota(jnp.int32, (fresh, keys), 0)
    causal = (column >= prefix) & (column - prefix <= row)
    ones = jnp.ones((keys, HEAD_SIZE), jnp.bfloat16)
    for b in range(block):
        split_ref[b, :earlier_rows] = earlier_ref[b].astype(jnp.float32)
        split_ref[b, earlier_rows : earlier_rows + fresh_rows] = stretch_ref[b].astype(jnp.float32)
        key = split_ref[b, pl.ds(0, keys, stride=2), :].astype(jnp.bfloat16)
        value = split_ref[b, pl.ds(1, keys, stride=2), :].astype(jnp.bfloat16)
        value = jnp.concatenate([value, ones], axis=1)
        limit = jnp.minimum(pos_ref[step * block + b], prefix)
        bias = jnp.where((column < limit) | causal, 0.0, MASKED)
        rows = slice(b * fresh, (b + 1) * fresh)
        query = jnp.concatenate(
            [query_ref[rows, h * HEAD_SIZE : (h + 1) * HEAD_SIZE] for h in range(heads)], axis=0
        )
        scores = lax.dot_general(query, key, CONTRACT_LAST, preferred_element_type=jnp.float32)
        scores = scores.reshape(heads, fresh, keys) * SCORE_SCALE + bias[None]
        top = jnp.max(scores, axis=-1, keepdims=True)
        weights = jnp.exp2(scores - top).astype(jnp.bfloat16).reshape(heads * fresh, keys)
        mixed = jnp.dot(weights, value, preferred_element_type=jnp.float32)
        result = (mixed[:, :HEAD_SIZE] / mixed[:, HEAD_SIZE:]).astype(jnp.bfloat16)
        for h in range(heads):
            out_ref[rows, h * HEAD_SIZE : (h + 1) * HEAD_SIZE] = result[
                h * fresh : (h + 1) * fresh
            ]


def prefill(position, query, earlier, stretch):
    prompts, earlier_rows, _ = earlier.shape
    fresh_rows = stretch.shape[1]
    width = query.shape[1]
    block = min(PROMPT_BLOCK, prompts)
    keys = -(-(earlier_rows + fresh_rows) // 2 // 256) * 256
    rows = block * fresh_rows // 2
    return pl.pallas_call(
        prefill_kernel,
        grid=(prompts // block,),
        out_shape=jax.ShapeDtypeStruct(query.shape, jnp.bfloat16),
        in_specs=[
            in_smem(),
            pl.BlockSpec((rows, width), lambda i: (i, 0)),
            pl.BlockSpec((block, earlier_rows, HEAD_SIZE), lambda i: (i, 0, 0)),
            pl.BlockSpec((block, fresh_rows, HEAD_SIZE), lambda i: (i, 0, 0)),
        ],
        out_specs=pl.BlockSpec((rows, width), lambda i: (i, 0)),
        scratch_shapes=[pltpu.VMEM((block, 2 * keys, HEAD_SIZE), jnp.float32)],
        compiler_params=params(),
        cost_estimate=cost(
            query.size * keys * 6,
            (2 * query.size + earlier.size + stretch.size) * 2,
            query.size // HEAD_SIZE * keys,
        ),
        name="prefill",
    )(position, query, earlier, stretch)


def down_kernel(input_ref, weight_ref, adapter_ref, out_ref):
    rows = input_ref.shape[0]
    span = 2 * ADAPTER_RANK
    wide = jnp.dot(input_ref[...], weight_ref[...], preferred_element_type=jnp.float32)
    owner = lax.broadcasted_iota(jnp.int32, wide.shape, 1) // span
    wide = jnp.where(owner == adapter_ref[...], wide, 0.0)
    folded = wide[:, :128] + wide[:, 128:]
    folded = folded + pltpu.roll(folded, 64, 1)
    folded = folded + pltpu.roll(folded, 32, 1)
    out_ref[...] = folded


def down(inputs, weight, adapter):
    rows, width = inputs.shape
    return pl.pallas_call(
        down_kernel,
        out_shape=jax.ShapeDtypeStruct((rows, 128), jnp.float32),
        in_specs=[in_vmem()] * 3,
        out_specs=in_vmem(),
        compiler_params=params(),
        cost_estimate=cost(2 * rows * width * 256, (inputs.size + weight.size) * 2),
        name="adapter_down",
    )(inputs, weight, adapter)


def sum_over_tensor(x):
    count = lax.axis_size("tensor")
    stride = 1
    while stride < count:
        x = x + lax.ppermute(x, "tensor", [(i, i ^ stride) for i in range(count)])
        stride *= 2
    return x


def attend(query, key, value, bias, top, total):
    rows, n = bias.shape
    heads = query.shape[0] // rows
    scores = lax.dot_general(query, key, CONTRACT_LAST, preferred_element_type=jnp.float32)
    scores = (scores.reshape(heads, rows, n) * SCORE_SCALE + bias[None]).reshape(heads * rows, n)
    new_top = jnp.maximum(top, jnp.max(scores, axis=-1, keepdims=True))
    weights = jnp.exp2(scores - new_top).astype(jnp.bfloat16)
    mixed = jnp.dot(weights, value, preferred_element_type=jnp.float32)
    return new_top, total * jnp.exp2(top - new_top) + mixed


def heads_of(ref, first, count):
    return jnp.concatenate(
        [ref[:, h * HEAD_SIZE : (h + 1) * HEAD_SIZE] for h in range(first, first + count)], axis=0
    )


def with_ones(value):
    return jnp.concatenate([value, jnp.ones_like(value)], axis=1)


def page_bias(table_ref, length_ref, page, offset):
    positions = table_ref.shape[1]
    length = length_ref[...]
    last = (length - 1) // PAGE
    times = jnp.zeros((length.shape[0], page.shape[1]), jnp.float32)
    tail_page = jnp.zeros_like(length)
    for p in range(positions):
        named = table_ref[:, p : p + 1]
        times = times + jnp.where(page == jnp.where(last > p, named, -1), 1.0, 0.0)
        tail_page = tail_page + jnp.where(last == p, named, 0)
    in_tail = (page == tail_page) & (offset < length - last * PAGE)
    times = times + jnp.where(in_tail, 1.0, 0.0)
    return jnp.where(times > 0.0, jnp.log2(jnp.maximum(times, 1.0)), MASKED)


def pool_kernel(
    query_ref, pool_ref, table_ref, length_ref, adapter_ref, middle_ref, up_ref, base_ref,
    attended_ref, level_ref, bias_ref, pool_bias_ref, split_ref, base_split_ref,
):
    rows = query_ref.shape[0]
    heads = query_ref.shape[1] // HEAD_SIZE
    pool_tokens = pool_ref.shape[0] // 2
    span = 2 * ADAPTER_RANK
    middle = middle_ref[...]
    middle = jnp.concatenate([middle, middle], axis=1)
    lane = lax.broadcasted_iota(jnp.int32, middle.shape, 1)
    mine = (lane // span) == adapter_ref[...]
    half = (lane % span) // ADAPTER_RANK
    base_split_ref[...] = base_ref[...].astype(jnp.float32)
    fresh = []
    for j in range(2):
        picked = jnp.where(mine & (half == j), middle, 0.0).astype(jnp.bfloat16)
        delta = jnp.dot(picked, up_ref[...], preferred_element_type=jnp.float32)
        base = base_split_ref[pl.ds(j, rows, stride=2), :]
        fresh.append((base + ADAPTER_SCALE * delta).astype(jnp.bfloat16).astype(jnp.float32))
    token = lax.broadcasted_iota(jnp.int32, (1, bias_ref.shape[1]), 1)
    page = (pool_tokens + token) // PAGE
    bias_ref[...] = page_bias(table_ref, length_ref, page, token % PAGE)
    token = lax.broadcasted_iota(jnp.int32, (1, pool_tokens), 1)
    pool_bias_ref[...] = page_bias(table_ref, length_ref, token // PAGE, token % PAGE)
    split_ref[...] = pool_ref[...].astype(jnp.float32)
    key = split_ref[pl.ds(0, pool_tokens, stride=2), :].astype(jnp.bfloat16)
    value = with_ones(split_ref[pl.ds(1, pool_tokens, stride=2), :].astype(jnp.bfloat16))
    own_total = with_ones(fresh[1])
    blocks = 2
    tokens = pool_tokens // blocks
    for first in range(0, heads, HEAD_BLOCK):
        query = heads_of(query_ref, first, HEAD_BLOCK)
        own = query.astype(jnp.float32) * jnp.concatenate([fresh[0]] * HEAD_BLOCK, axis=0)
        top = jnp.sum(own, axis=-1, keepdims=True) * SCORE_SCALE
        total = jnp.concatenate([own_total] * HEAD_BLOCK, axis=0)
        for c in range(blocks):
            block = slice(c * tokens, (c + 1) * tokens)
            top, total = attend(query, key[block], value[block], pool_bias_ref[:, block], top, total)
        attended_ref[first * rows : (first + HEAD_BLOCK) * rows] = total[:, :HEAD_SIZE] / total[:, HEAD_SIZE:]
        level = top + jnp.log2(total[:, HEAD_SIZE : HEAD_SIZE + 1])
        for h in range(HEAD_BLOCK):
            level_ref[:, first + h : first + h + 1] = level[h * rows : (h + 1) * rows]


def pool_decode(query, pool, table, length, adapter, middle, up, base, landing_tokens):
    rows, width = query.shape
    stacked = rows * width // HEAD_SIZE
    pool_tokens = pool.shape[0] // 2
    return pl.pallas_call(
        pool_kernel,
        out_shape=(
            jax.ShapeDtypeStruct((stacked, HEAD_SIZE), jnp.float32),
            jax.ShapeDtypeStruct((rows, stacked // rows), jnp.float32),
            jax.ShapeDtypeStruct((rows, landing_tokens), jnp.float32),
        ),
        in_specs=[in_vmem()] * 8,
        out_specs=[in_vmem()] * 3,
        scratch_shapes=[
            pltpu.VMEM((rows, pool_tokens), jnp.float32),
            pltpu.VMEM(pool.shape, jnp.float32),
            pltpu.VMEM(base.shape, jnp.float32),
        ],
        compiler_params=params(),
        cost_estimate=cost(
            stacked * pool_tokens * HEAD_SIZE * 6, pool.size * 2 + stacked * 1536, stacked * pool_tokens
        ),
        name="pool_decode",
    )(query, pool, table, length, adapter, middle, up, base)


def landing_kernel(query_ref, landing_ref, bias_ref, attended_ref, level_ref, out_ref):
    rows = query_ref.shape[0]
    heads = query_ref.shape[1] // HEAD_SIZE
    groups, cap, slot_rows, _ = landing_ref.shape
    half = slot_rows // 2
    span = min(groups, LANDING_TOKENS // (cap * half))
    tokens = span * cap * half
    for first in range(0, heads, HEAD_BLOCK):
        query = heads_of(query_ref, first, HEAD_BLOCK)
        top = jnp.concatenate(
            [level_ref[:, h : h + 1] for h in range(first, first + HEAD_BLOCK)], axis=0
        )
        total = with_ones(attended_ref[first * rows : (first + HEAD_BLOCK) * rows])
        for c in range(groups // span):
            block = slice(c * span, (c + 1) * span)
            key = landing_ref[block, :, :half].reshape(tokens, HEAD_SIZE)
            value = with_ones(landing_ref[block, :, half:].reshape(tokens, HEAD_SIZE))
            bias = bias_ref[:, c * tokens : (c + 1) * tokens]
            top, total = attend(query, key, value, bias, top, total)
        result = (total[:, :HEAD_SIZE] / total[:, HEAD_SIZE:]).astype(jnp.bfloat16)
        for h in range(HEAD_BLOCK):
            lanes = slice((first + h) * HEAD_SIZE, (first + h + 1) * HEAD_SIZE)
            out_ref[:, lanes] = result[h * rows : (h + 1) * rows]


def landing_decode(query, landing, bias, attended, level):
    stacked = attended.shape[0]
    tokens = bias.shape[1]
    return pl.pallas_call(
        landing_kernel,
        out_shape=jax.ShapeDtypeStruct(query.shape, jnp.bfloat16),
        in_specs=[in_vmem()] * 5,
        out_specs=in_vmem(),
        compiler_params=params(),
        cost_estimate=cost(
            stacked * tokens * HEAD_SIZE * 6, landing.size * 2 + stacked * 1024, stacked * tokens
        ),
        name="landing_decode",
    )(query, landing, bias, attended, level)


def body(
    stretch_query_rows,
    earlier_token_cache,
    stretch_cache,
    stretch_position,
    owning_decode_group,
    decode_query_rows,
    decode_input_rows,
    decode_base_projection,
    row_adapter_index,
    adapter_down_weight,
    adapter_up_weight,
    group_page_store,
    row_page_index,
    cached_token_length,
):
    groups = lax.axis_size("group")
    prompts, stretch_len = stretch_cache.shape[:2]
    prefix_len = earlier_token_cache.shape[1]
    stretch = stretch_cache.reshape(prompts, 2 * stretch_len, HEAD_SIZE)
    earlier = earlier_token_cache.reshape(prompts, 2 * prefix_len, HEAD_SIZE)
    pool = group_page_store.reshape(-1, HEAD_SIZE)
    base = decode_base_projection.reshape(-1, HEAD_SIZE)
    adapter = row_adapter_index[:, None]
    length = cached_token_length[:, None]

    outgoing = pack(owning_decode_group, stretch, groups)
    landing = lax.all_to_all(
        outgoing.reshape(groups, -1, HEAD_SIZE), "group", 0, 0, tiled=True
    ).reshape(outgoing.shape)
    middle = sum_over_tensor(down(decode_input_rows, adapter_down_weight, adapter))
    prefill_out = prefill(stretch_position, stretch_query_rows, earlier, stretch)
    attended, level, bias = pool_decode(
        decode_query_rows, pool, row_page_index, length, adapter, middle, adapter_up_weight, base,
        groups * CAP * stretch_len,
    )
    decode_out = landing_decode(decode_query_rows, landing, bias, attended, level)
    return (prefill_out, decode_out)


def solution(mesh):
    placed = (
        P("group", "tensor"),
        P("group", None, None, "tensor"),
        P("group", None, None, "tensor"),
        P("group"),
        P("group"),
        P("group", "tensor"),
        P("group", "tensor"),
        P("group", None, "tensor"),
        P("group"),
        P("tensor", None),
        P(None, "tensor"),
        P("group", None, None, "tensor"),
        P("group", None),
        P("group"),
    )
    return jax.shard_map(
        body,
        mesh=mesh,
        in_specs=placed,
        out_specs=(P("group", "tensor"), P("group", "tensor")),
        check_vma=False,
    )
```

time: 266 us -> 57.6 us (0.22)
  waiting for transfers between devices: 80.3 us -> 20.4 us
  matrix products: 57.1 us -> 0 us
  local copies, waits for them, and re-layouts: 54.4 us -> 5.23 us
  blocking collectives: 46 us -> 0 us
  Pallas kernels: 0 us -> 16.5 us
  between operations: 15.1 us -> 0.78 us
  starting transfers between devices: 0.04 us -> 14.2 us
  other arithmetic: 11.6 us -> 0.02 us
    all_gather x1 -> x0, waiting for transfers between devices: 80.3 us -> none  [body(): piece_cache = lax.all_gather(stretch_flat, 'group', axis=0, tiled=True)]
    dot_general x12 -> x0, matrix products: 57.1 us -> none  [the longest x1 13.8 us: body(): landed = jnp.dot(placement, piece_cache, preferred_element_type=jnp.float32)]
    unnamed x1 -> x0, blocking collectives: 24.1 us -> none
    slice x5 -> x0, local copies, waits for them, and re-layouts: 23.6 us -> none  [the longest x2 16.4 us: decode_part(): collected_pages[:, :, :, 0]]
    psum x1 -> x0, blocking collectives: 21.8 us -> none  [adapter_correction(): summed = lax.psum(picked, 'tensor')]
    reshape x3 -> x0, local copies, waits for them, and re-layouts: 19.3 us -> none  [the longest x1 13.6 us: decode_part(): collected_sum.astype(jnp.bfloat16)]
    pallas_call x0 -> x5, Pallas kernels: none -> 16.5 us  [the longest x1 6.65 us: prefill(): pl.pallas_call(prefill_kernel, grid=(prompts // block,), out_shape=jax.Sh...]
    all_to_all x0 -> x1, waiting for transfers between devices: none -> 15.9 us  [body(): lax.all_to_all(outgoing.reshape(groups, -1, HEAD_SIZE), 'group', 0, 0, ti...]
  transfers between devices with their start and end apart: 1 -> 4, of which waited for: 1 -> 3; matrix products, arithmetic and copies ran while one was open for 23% -> 1% of each run, Pallas kernels for 0% -> 19%
where the time goes in v1:
time: 57.6 us; the launch traced here: 57.3 us
  waiting for transfers between devices  20.4 us (35%)
  Pallas kernels  16.5 us (29%)
  starting transfers between devices  14.2 us (25%)
  local copies, waits for them, and re-layouts  5.23 us (9%)
  between operations  0.78 us (1%)
    all_to_all x1, waiting for transfers between devices, body(): lax.all_to_all(outgoing.reshape(groups, -1, HEAD_SIZE), 'group', 0, 0, ti...  15.9 us
    all_to_all x1, starting transfers between devices, body(): lax.all_to_all(outgoing.reshape(groups, -1, HEAD_SIZE), 'group', 0, 0, ti...  11.5 us
    pallas_call x1, Pallas kernels, prefill(): pl.pallas_call(prefill_kernel, grid=(prompts // block,), out_shape=jax.Sh...  6.65 us
    unnamed x27, local copies, waits for them, and re-layouts  5.04 us
    ppermute x3, waiting for transfers between devices, sum_over_tensor(): x = x + lax.ppermute(x, 'tensor', [(i, i ^ stride) for i in range(count)])  4.58 us
    pallas_call x1, Pallas kernels, pool_decode(): pl.pallas_call(pool_kernel, out_shape=(jax.ShapeDtypeStruct((stacked, HEA...  3.81 us
    pallas_call x1, Pallas kernels, landing_decode(): pl.pallas_call(landing_kernel, out_shape=jax.ShapeDtypeStruct(query.shape...  3.34 us
    ppermute x3, starting transfers between devices, sum_over_tensor(): x = x + lax.ppermute(x, 'tensor', [(i, i ^ stride) for i in range(count)])  2.75 us
  transfers between devices with their start and end apart: 4, of which 3 were waited for; matrix products, arithmetic and copies ran while one was open for 1% of the time, Pallas kernels for 19%

profile of v1, /device:TPU:2, one launch (start us, length us, event | category | flops | bytes accessed | tf_op | source)
XLA Modules:
  0.0 57.3 jit_solution(7260599322645058258)
XLA Ops:
  0.6 0.0 copy-start.11
  0.6 0.0 copy-start.3
  0.7 0.0 copy-start.4
  0.7 0.0 copy-start
  0.7 0.0 copy-start.5
  0.7 2.4 %pack.1 = bf16[32,2,96,128]{3,2,1,0:T(8,128)(2,1)} custom-call(s32[32]{0:T(128)} %owner_hbm.1, bf16[32,96,128]{2,1,0:T(8,128)(2,1)} %bitcast.8), custom_call_target="tpu_custom_call" | custom-call | bytes 2359296 | tf_op jit(solution)/shard_map/pack/pallas_call | solution.py:96
  3.1 11.5 %all-to-all-start = ((bf16[32,192,128]{2,1,0:T(8,128)(2,1)}), bf16[32,192,128]{2,1,0:T(8,128)(2,1)S(1)}, u32[]{:S(2)}, u32[]{:S(2)}) async-start(bf16[32,192,128]{2,1,0:T(8,128)(2,1)} %bitcast.14), calls=%async_computation | async-start | bytes 3145728 | tf_op jit(solution)/shard_map/all_to_all | solution.py:397
  14.6 0.0 copy-done.11
  14.6 0.1 copy.19.adapter_ref
  14.7 0.0 copy-done.3
  14.7 0.0 copy-done.4
  14.7 0.3 adapter_down.1
  15.0 0.1 collective-permute-start
  15.1 1.2 %collective-permute-done = f32[64,128]{1,0:T(8,128)S(1)} collective-permute-done((f32[64,128]{1,0:T(8,128)S(1)}, f32[64,128]{1,0:T(8,128)S(1)}, u32[]{:S(2)}, u32[]{:S(2)}) %collective-permute-start) | collective-permute-done | bytes 32800 | tf_op jit(solution)/shard_map/ppermute | solution.py:217
  16.3 0.5 collective-permute-start.1
  16.9 3.4 %collective-permute-done.1 = f32[64,128]{1,0:T(8,128)S(1)} collective-permute-done((f32[64,128]{1,0:T(8,128)S(1)}, f32[64,128]{1,0:T(8,128)S(1)}, u32[]{:S(2)}, u32[]{:S(2)}) %collective-permute-start.1) | collective-permute-done | bytes 32800 | tf_op jit(solution)/shard_map/ppermute | solution.py:217
  20.3 2.1 %collective-permute-start.2 = (f32[64,128]{1,0:T(8,128)S(1)}, f32[64,128]{1,0:T(8,128)S(1)}, u32[]{:S(2)}, u32[]{:S(2)}) collective-permute-start(f32[64,128]{1,0:T(8,128)S(1)} %add.10), channel_id=1, source_target_pairs={{0,4},{1,5},{2,6},{3,7},{4,0},{5,1},{6,2},{7,3},{8,12},{9,13},{10,... | collective-permute-start | bytes 98312 | tf_op jit(solution)/shard_map/ppermute | solution.py:217
  22.4 0.0 copy-done
  22.4 0.0 copy-done.5
  22.4 1.9 %copy-done.1 = bf16[1536,1024]{1,0:T(8,128)(2,1)S(1)} copy-done((bf16[1536,1024]{1,0:T(8,128)(2,1)S(1)}, bf16[1536,1024]{1,0:T(8,128)(2,1)}, u32[]{:S(2)}) %copy-start.1) | copy-done | bytes 3145752
  24.3 1.9 %copy-done.2 = bf16[32,192,2,128]{3,2,1,0:T(2,128)(2,1)S(1)} copy-done((bf16[32,192,2,128]{3,2,1,0:T(2,128)(2,1)S(1)}, bf16[32,192,2,128]{3,2,1,0:T(2,128)(2,1)}, u32[]{:S(2)}) %copy-start.2) | copy-done | bytes 3145752
  26.2 0.0 copy-start.9
  26.2 6.6 %prefill.1 = bf16[1536,1024]{1,0:T(8,128)(2,1)} custom-call(s32[32]{0:T(128)S(1)} %copy-done.5, bf16[1536,1024]{1,0:T(8,128)(2,1)S(1)} %copy-done.1, bf16[32,384,128]{2,1,0:T(8,128)(2,1)S(1)} %bitcast.10, bf16[32,96,128]{2,1,0:T(8,128)(2,1)S(1)} %bitcast.9), custom_call_target="tpu_custom_call" | custom-call | flops 2415919104 | bytes 10223616 | tf_op jit(solution)/shard_map/prefill/pallas_call | solution.py:166
  32.8 0.1 copy.17.table_ref
  32.9 0.0 copy-done.12
  32.9 0.1 copy.18.length_ref
  33.0 0.0 collective-permute-done.2
  33.1 0.0 copy-start.6
  33.1 1.1 %copy-done.6 = bf16[96,16,2,128]{3,2,1,0:T(2,128)(2,1)S(1)} copy-done((bf16[96,16,2,128]{3,2,1,0:T(2,128)(2,1)S(1)}, bf16[96,16,2,128]{3,2,1,0:T(2,128)(2,1)}, u32[]{:S(2)}) %copy-start.6) | copy-done | bytes 786456
  34.2 3.8 %pool_decode.1 = (f32[512,128]{1,0:T(8,128)S(1)}, f32[64,8]{1,0:T(8,128)S(1)}, f32[64,3072]{1,0:T(8,128)S(1)}) custom-call(bf16[64,1024]{1,0:T(8,128)(2,1)S(1)} %copy-done.7, bf16[3072,128]{1,0:T(8,128)(2,1)S(1)} %bitcast.12, s32[64,15]{1,0:T(8,128)S(1)} %copy.17.table_ref, s32[64,1]{1,0:T(8,128)S(1)} %copy.18.length_ref, s32[64,1]{1,0:T(8,128)S(1)} %copy.19.adapter_ref, ...), custom_call_target="tpu_custom_call" | custom-call | flops 603979776 | bytes 1572864 | tf_op jit(solution)/shard_map/pool_decode/pallas_call | solution.py:307
  38.0 15.9 %all-to-all-done = bf16[32,192,128]{2,1,0:T(8,128)(2,1)S(1)} async-done(((bf16[32,192,128]{2,1,0:T(8,128)(2,1)}), bf16[32,192,128]{2,1,0:T(8,128)(2,1)S(1)}, u32[]{:S(2)}, u32[]{:S(2)}) %all-to-all-start) | async-done | bytes 1572896 | tf_op jit(solution)/shard_map/all_to_all | solution.py:397
  53.9 3.3 %landing_decode.1 = bf16[64,1024]{1,0:T(8,128)(2,1)} custom-call(bf16[64,1024]{1,0:T(8,128)(2,1)S(1)} %copy-done.7, bf16[32,2,96,128]{3,2,1,0:T(8,128)(2,1)S(1)} %bitcast.11, f32[64,3072]{1,0:T(8,128)S(1)} %get-tuple-element.5.bias_ref, f32[512,128]{1,0:T(8,128)S(1)} %get-tuple-element.6.attended_ref, f32[64,8]{1,0:T(8,128)S(1)} %get-tuple-element.7.level_ref), custom_call_target="tpu_custom_call" | custom-call | flops 1207959552 | bytes 2097152 | tf_op jit(solution)/shard_map/landing_decode/pallas_call | solution.py:357
  (13 shorter events, 0.0 us)
Async XLA Ops:
  0.6 13.9 %copy-start.11 = (s32[64]{0:T(128)S(1)}, s32[64]{0:T(128)}, u32[]{:S(2)}) copy-start(s32[64]{0:T(128)} %param.22) | copy-start | bytes 772
  0.6 14.0 %copy-start.3 = (bf16[1024,256]{1,0:T(8,128)(2,1)S(1)}, bf16[1024,256]{1,0:T(8,128)(2,1)}, u32[]{:S(2)}) copy-start(bf16[1024,256]{1,0:T(8,128)(2,1)} %weight_ref.1) | copy-start | bytes 1572868
  0.7 14.0 %copy-start.4 = (bf16[64,1024]{1,0:T(8,128)(2,1)S(1)}, bf16[64,1024]{1,0:T(8,128)(2,1)}, u32[]{:S(2)}) copy-start(bf16[64,1024]{1,0:T(8,128)(2,1)} %input_ref.1) | copy-start | bytes 393220
  0.7 21.7 %copy-start = (bf16[32,48,2,128]{3,2,1,0:T(2,128)(2,1)S(1)}, bf16[32,48,2,128]{3,2,1,0:T(2,128)(2,1)}, u32[]{:S(2)}) copy-start(bf16[32,48,2,128]{3,2,1,0:T(2,128)(2,1)} %param.16) | copy-start | bytes 2359300
  0.7 21.7 %copy-start.5 = (s32[32]{0:T(128)S(1)}, s32[32]{0:T(128)}, u32[]{:S(2)}) copy-start(s32[32]{0:T(128)} %pos_ref.1) | copy-start | bytes 388
  3.1 50.8 %all-to-all-start = ((bf16[32,192,128]{2,1,0:T(8,128)(2,1)}), bf16[32,192,128]{2,1,0:T(8,128)(2,1)S(1)}, u32[]{:S(2)}, u32[]{:S(2)}) async-start(bf16[32,192,128]{2,1,0:T(8,128)(2,1)} %bitcast.14), calls=%async_computation | async-start | bytes 3145728 | tf_op jit(solution)/shard_map/all_to_all | solution.py:397
  15.0 1.3 %collective-permute-start = (f32[64,128]{1,0:T(8,128)S(1)}, f32[64,128]{1,0:T(8,128)S(1)}, u32[]{:S(2)}, u32[]{:S(2)}) collective-permute-start(f32[64,128]{1,0:T(8,128)S(1)} %adapter_down.1), channel_id=1, source_target_pairs={{0,1},{1,0},{2,3},{3,2},{4,5},{5,4},{6,7},{7,6},{8,9},{9,8},{10,11... | collective-permute-start | bytes 98312 | tf_op jit(solution)/shard_map/ppermute | solution.py:217
  16.3 3.9 %collective-permute-start.1 = (f32[64,128]{1,0:T(8,128)S(1)}, f32[64,128]{1,0:T(8,128)S(1)}, u32[]{:S(2)}, u32[]{:S(2)}) collective-permute-start(f32[64,128]{1,0:T(8,128)S(1)} %add.9), channel_id=1, source_target_pairs={{0,2},{1,3},{2,0},{3,1},{4,6},{5,7},{6,4},{7,5},{8,10},{9,11},{10,... | collective-permute-start | bytes 98312 | tf_op jit(solution)/shard_map/ppermute | solution.py:217
  20.3 12.8 %collective-permute-start.2 = (f32[64,128]{1,0:T(8,128)S(1)}, f32[64,128]{1,0:T(8,128)S(1)}, u32[]{:S(2)}, u32[]{:S(2)}) collective-permute-start(f32[64,128]{1,0:T(8,128)S(1)} %add.10), channel_id=1, source_target_pairs={{0,4},{1,5},{2,6},{3,7},{4,0},{5,1},{6,2},{7,3},{8,12},{9,13},{10,... | collective-permute-start | bytes 98312 | tf_op jit(solution)/shard_map/ppermute | solution.py:217
  22.4 1.9 %copy-start.1 = (bf16[1536,1024]{1,0:T(8,128)(2,1)S(1)}, bf16[1536,1024]{1,0:T(8,128)(2,1)}, u32[]{:S(2)}) copy-start(bf16[1536,1024]{1,0:T(8,128)(2,1)} %query_ref.3) | copy-start | bytes 9437188
  24.3 1.9 %copy-start.2 = (bf16[32,192,2,128]{3,2,1,0:T(2,128)(2,1)S(1)}, bf16[32,192,2,128]{3,2,1,0:T(2,128)(2,1)}, u32[]{:S(2)}) copy-start(bf16[32,192,2,128]{3,2,1,0:T(2,128)(2,1)} %param.15) | copy-start | bytes 9437188
  26.2 6.7 %copy-start.10 = (s32[64,15]{0,1:T(8,128)S(1)}, s32[64,15]{0,1:T(8,128)}, u32[]{:S(2)}) copy-start(s32[64,15]{0,1:T(8,128)} %param.26) | copy-start | bytes 11524
  26.2 6.8 %copy-start.12 = (s32[64]{0:T(128)S(1)}, s32[64]{0:T(128)}, u32[]{:S(2)}) copy-start(s32[64]{0:T(128)} %param.27) | copy-start | bytes 772
  26.2 6.9 %copy-start.7 = (bf16[64,1024]{1,0:T(8,128)(2,1)S(1)}, bf16[64,1024]{1,0:T(8,128)(2,1)}, u32[]{:S(2)}) copy-start(bf16[64,1024]{1,0:T(8,128)(2,1)} %query_ref.5) | copy-start | bytes 393220
  26.2 6.9 %copy-start.8 = (bf16[256,128]{1,0:T(8,128)(2,1)S(1)}, bf16[256,128]{1,0:T(8,128)(2,1)}, u32[]{:S(2)}) copy-start(bf16[256,128]{1,0:T(8,128)(2,1)} %up_ref.1) | copy-start | bytes 196612
  26.2 6.9 %copy-start.9 = (bf16[64,2,128]{2,1,0:T(2,128)(2,1)S(1)}, bf16[64,2,128]{2,1,0:T(2,128)(2,1)}, u32[]{:S(2)}) copy-start(bf16[64,2,128]{2,1,0:T(2,128)(2,1)} %param.21) | copy-start | bytes 98308
  33.1 1.1 %copy-start.6 = (bf16[96,16,2,128]{3,2,1,0:T(2,128)(2,1)S(1)}, bf16[96,16,2,128]{3,2,1,0:T(2,128)(2,1)}, u32[]{:S(2)}) copy-start(bf16[96,16,2,128]{3,2,1,0:T(2,128)(2,1)} %param.25) | copy-start | bytes 2359300

commit v2 on v1

--- a/solution.py
+++ b/solution.py
@@ -20,6 +20,7 @@
 PROMPT_BLOCK = 8
 HEAD_BLOCK = 4
 LANDING_TOKENS = 768
+SAFE_TOTAL = 2.0**100
 
 CONTRACT_LAST = (((1,), (1,)), ((), ()))
 
@@ -68,6 +69,17 @@
         rank = count_ref[dest]
         count_ref[dest] = rank + 1
         slot_ref[p] = jnp.minimum(rank, cap - 1)
+    for d in range(groups):
+        held = count_ref[d]
+        for taken in range(cap):
+
+            @pl.when(held == taken)
+            def _():
+                rest = pl.ds(0, cap - taken)
+                pltpu.make_async_copy(
+                    zero_ref.at[rest], out_hbm.at[d, pl.ds(taken, cap - taken)], out_sem
+                ).start()
+
     for c in range(parts):
         kv_copies[c].wait()
         block = slice(c * span, (c + 1) * span)
@@ -80,13 +92,6 @@
             pltpu.make_async_copy(
                 stage_ref.at[p], out_hbm.at[owner_ref[p], slot_ref[p]], out_sem
             ).start()
-    for d in range(groups):
-        for slot in range(cap):
-
-            @pl.when(count_ref[d] <= slot)
-            def _():
-                pltpu.make_async_copy(zero_ref, out_hbm.at[d, slot], out_sem).start()
-
     pltpu.make_async_copy(out_hbm, out_hbm, out_sem).wait()
 
 
@@ -103,7 +108,7 @@
             pltpu.VMEM(stretch.shape, jnp.bfloat16),
             pltpu.VMEM(stretch.shape, jnp.float32),
             pltpu.VMEM(stretch.shape, jnp.bfloat16),
-            pltpu.VMEM((rows, HEAD_SIZE), jnp.bfloat16),
+            pltpu.VMEM((CAP, rows, HEAD_SIZE), jnp.bfloat16),
             pltpu.SMEM((groups,), jnp.int32),
             pltpu.SMEM((prompts,), jnp.int32),
             pltpu.SemaphoreType.DMA,
@@ -333,22 +338,46 @@
     half = slot_rows // 2
     span = min(groups, LANDING_TOKENS // (cap * half))
     tokens = span * cap * half
-    for first in range(0, heads, HEAD_BLOCK):
+
+    def begin(first):
         query = heads_of(query_ref, first, HEAD_BLOCK)
         top = jnp.concatenate(
             [level_ref[:, h : h + 1] for h in range(first, first + HEAD_BLOCK)], axis=0
         )
-        total = with_ones(attended_ref[first * rows : (first + HEAD_BLOCK) * rows])
-        for c in range(groups // span):
-            block = slice(c * span, (c + 1) * span)
-            key = landing_ref[block, :, :half].reshape(tokens, HEAD_SIZE)
-            value = with_ones(landing_ref[block, :, half:].reshape(tokens, HEAD_SIZE))
-            bias = bias_ref[:, c * tokens : (c + 1) * tokens]
-            top, total = attend(query, key, value, bias, top, total)
+        return query, top, with_ones(attended_ref[first * rows : (first + HEAD_BLOCK) * rows])
+
+    def part(c):
+        block = slice(c * span, (c + 1) * span)
+        key = landing_ref[block, :, :half].reshape(tokens, HEAD_SIZE)
+        value = with_ones(landing_ref[block, :, half:].reshape(tokens, HEAD_SIZE))
+        return key, value, bias_ref[:, c * tokens : (c + 1) * tokens]
+
+    def finish(first, total):
         result = (total[:, :HEAD_SIZE] / total[:, HEAD_SIZE:]).astype(jnp.bfloat16)
         for h in range(HEAD_BLOCK):
             lanes = slice((first + h) * HEAD_SIZE, (first + h + 1) * HEAD_SIZE)
             out_ref[:, lanes] = result[h * rows : (h + 1) * rows]
+
+    worst = jnp.zeros((8, HEAD_SIZE), jnp.float32)
+    for first in range(0, heads, HEAD_BLOCK):
+        query, top, total = begin(first)
+        top = top.reshape(HEAD_BLOCK, rows, 1)
+        for c in range(groups // span):
+            key, value, bias = part(c)
+            scores = lax.dot_general(query, key, CONTRACT_LAST, preferred_element_type=jnp.float32)
+            scores = scores.reshape(HEAD_BLOCK, rows, tokens) * SCORE_SCALE + (bias[None] - top)
+            weights = jnp.exp2(scores).astype(jnp.bfloat16).reshape(HEAD_BLOCK * rows, tokens)
+            total = total + jnp.dot(weights, value, preferred_element_type=jnp.float32)
+        finish(first, total)
+        worst = jnp.maximum(worst, jnp.max(total[:, HEAD_SIZE:].reshape(-1, 8, HEAD_SIZE), axis=0))
+
+    @pl.when(jnp.logical_not(jnp.max(worst) < SAFE_TOTAL))
+    def _():
+        for first in range(0, heads, HEAD_BLOCK):
+            query, top, total = begin(first)
+            for c in range(groups // span):
+                top, total = attend(query, *part(c), top, total)
+            finish(first, total)
 
 
 def landing_decode(query, landing, bias, attended, level):

time: 57.6 us -> 56.9 us (0.988)
  Pallas kernels: 16.5 us -> 15.8 us
where the time goes in v2:
time: 56.9 us; the launch traced here: 56.6 us
  waiting for transfers between devices  20.4 us (36%)
  Pallas kernels  15.8 us (28%)
  starting transfers between devices  14.3 us (25%)
  local copies, waits for them, and re-layouts  5.23 us (9%)
  between operations  0.78 us (1%)
    all_to_all x1, waiting for transfers between devices, body(): lax.all_to_all(outgoing.reshape(groups, -1, HEAD_SIZE), 'group', 0, 0, ti...  15.9 us
    all_to_all x1, starting transfers between devices, body(): lax.all_to_all(outgoing.reshape(groups, -1, HEAD_SIZE), 'group', 0, 0, ti...  11.5 us
    pallas_call x1, Pallas kernels, prefill(): pl.pallas_call(prefill_kernel, grid=(prompts // block,), out_shape=jax.Sh...  6.65 us
    unnamed x27, local copies, waits for them, and re-layouts  5.04 us
    ppermute x3, waiting for transfers between devices, sum_over_tensor(): x = x + lax.ppermute(x, 'tensor', [(i, i ^ stride) for i in range(count)])  4.58 us
    pallas_call x1, Pallas kernels, pool_decode(): pl.pallas_call(pool_kernel, out_shape=(jax.ShapeDtypeStruct((stacked, HEA...  3.81 us
    pallas_call x1, Pallas kernels, landing_decode(): pl.pallas_call(landing_kernel, out_shape=jax.ShapeDtypeStruct(query.shape...  2.88 us
    ppermute x3, starting transfers between devices, sum_over_tensor(): x = x + lax.ppermute(x, 'tensor', [(i, i ^ stride) for i in range(count)])  2.75 us
  transfers between devices with their start and end apart: 4, of which 3 were waited for; matrix products, arithmetic and copies ran while one was open for 1% of the time, Pallas kernels for 19%

profile of v2, /device:TPU:2, one launch (start us, length us, event | category | flops | bytes accessed | tf_op | source)
XLA Modules:
  0.0 56.6 jit_solution(12503036172519454090)
XLA Ops:
  0.6 0.0 copy-start.11
  0.6 0.0 copy-start.3
  0.7 0.0 copy-start.4
  0.7 0.0 copy-start
  0.7 0.0 copy-start.5
  0.7 2.1 %pack.1 = bf16[32,2,96,128]{3,2,1,0:T(8,128)(2,1)} custom-call(s32[32]{0:T(128)} %owner_hbm.1, bf16[32,96,128]{2,1,0:T(8,128)(2,1)} %bitcast.8), custom_call_target="tpu_custom_call" | custom-call | bytes 2359296 | tf_op jit(solution)/shard_map/pack/pallas_call | solution.py:101
  2.8 11.5 %all-to-all-start = ((bf16[32,192,128]{2,1,0:T(8,128)(2,1)}), bf16[32,192,128]{2,1,0:T(8,128)(2,1)S(1)}, u32[]{:S(2)}, u32[]{:S(2)}) async-start(bf16[32,192,128]{2,1,0:T(8,128)(2,1)} %bitcast.14), calls=%async_computation | async-start | bytes 3145728 | tf_op jit(solution)/shard_map/all_to_all | solution.py:426
  14.3 0.0 copy-done.11
  14.4 0.1 copy.19.adapter_ref
  14.5 0.0 copy-done.3
  14.5 0.0 copy-done.4
  14.5 0.3 adapter_down.1
  14.8 0.1 collective-permute-start
  14.9 1.2 %collective-permute-done = f32[64,128]{1,0:T(8,128)S(1)} collective-permute-done((f32[64,128]{1,0:T(8,128)S(1)}, f32[64,128]{1,0:T(8,128)S(1)}, u32[]{:S(2)}, u32[]{:S(2)}) %collective-permute-start) | collective-permute-done | bytes 32800 | tf_op jit(solution)/shard_map/ppermute | solution.py:222
  16.1 0.5 collective-permute-start.1
  16.7 3.4 %collective-permute-done.1 = f32[64,128]{1,0:T(8,128)S(1)} collective-permute-done((f32[64,128]{1,0:T(8,128)S(1)}, f32[64,128]{1,0:T(8,128)S(1)}, u32[]{:S(2)}, u32[]{:S(2)}) %collective-permute-start.1) | collective-permute-done | bytes 32800 | tf_op jit(solution)/shard_map/ppermute | solution.py:222
  20.0 2.1 %collective-permute-start.2 = (f32[64,128]{1,0:T(8,128)S(1)}, f32[64,128]{1,0:T(8,128)S(1)}, u32[]{:S(2)}, u32[]{:S(2)}) collective-permute-start(f32[64,128]{1,0:T(8,128)S(1)} %add.10), channel_id=1, source_target_pairs={{0,4},{1,5},{2,6},{3,7},{4,0},{5,1},{6,2},{7,3},{8,12},{9,13},{10,... | collective-permute-start | bytes 98312 | tf_op jit(solution)/shard_map/ppermute | solution.py:222
  22.2 0.0 copy-done
  22.2 0.0 copy-done.5
  22.2 1.9 %copy-done.1 = bf16[1536,1024]{1,0:T(8,128)(2,1)S(1)} copy-done((bf16[1536,1024]{1,0:T(8,128)(2,1)S(1)}, bf16[1536,1024]{1,0:T(8,128)(2,1)}, u32[]{:S(2)}) %copy-start.1) | copy-done | bytes 3145752
  24.1 1.9 %copy-done.2 = bf16[32,192,2,128]{3,2,1,0:T(2,128)(2,1)S(1)} copy-done((bf16[32,192,2,128]{3,2,1,0:T(2,128)(2,1)S(1)}, bf16[32,192,2,128]{3,2,1,0:T(2,128)(2,1)}, u32[]{:S(2)}) %copy-start.2) | copy-done | bytes 3145752
  26.0 0.0 copy-start.9
  26.0 6.6 %prefill.1 = bf16[1536,1024]{1,0:T(8,128)(2,1)} custom-call(s32[32]{0:T(128)S(1)} %copy-done.5, bf16[1536,1024]{1,0:T(8,128)(2,1)S(1)} %copy-done.1, bf16[32,384,128]{2,1,0:T(8,128)(2,1)S(1)} %bitcast.10, bf16[32,96,128]{2,1,0:T(8,128)(2,1)S(1)} %bitcast.9), custom_call_target="tpu_custom_call" | custom-call | flops 2415919104 | bytes 10223616 | tf_op jit(solution)/shard_map/prefill/pallas_call | solution.py:171
  32.6 0.0 copy-done.10
  32.6 0.1 copy.17.table_ref
  32.7 0.1 copy.18.length_ref
  32.8 0.0 collective-permute-done.2
  32.9 0.0 copy-start.6
  32.9 1.1 %copy-done.6 = bf16[96,16,2,128]{3,2,1,0:T(2,128)(2,1)S(1)} copy-done((bf16[96,16,2,128]{3,2,1,0:T(2,128)(2,1)S(1)}, bf16[96,16,2,128]{3,2,1,0:T(2,128)(2,1)}, u32[]{:S(2)}) %copy-start.6) | copy-done | bytes 786456
  34.0 3.8 %pool_decode.1 = (f32[512,128]{1,0:T(8,128)S(1)}, f32[64,8]{1,0:T(8,128)S(1)}, f32[64,3072]{1,0:T(8,128)S(1)}) custom-call(bf16[64,1024]{1,0:T(8,128)(2,1)S(1)} %copy-done.7, bf16[3072,128]{1,0:T(8,128)(2,1)S(1)} %bitcast.12, s32[64,15]{1,0:T(8,128)S(1)} %copy.17.table_ref, s32[64,1]{1,0:T(8,128)S(1)} %copy.18.length_ref, s32[64,1]{1,0:T(8,128)S(1)} %copy.19.adapter_ref, ...), custom_call_target="tpu_custom_call" | custom-call | flops 603979776 | bytes 1572864 | tf_op jit(solution)/shard_map/pool_decode/pallas_call | solution.py:312
  37.8 15.9 %all-to-all-done = bf16[32,192,128]{2,1,0:T(8,128)(2,1)S(1)} async-done(((bf16[32,192,128]{2,1,0:T(8,128)(2,1)}), bf16[32,192,128]{2,1,0:T(8,128)(2,1)S(1)}, u32[]{:S(2)}, u32[]{:S(2)}) %all-to-all-start) | async-done | bytes 1572896 | tf_op jit(solution)/shard_map/all_to_all | solution.py:426
  53.7 2.9 %landing_decode.1 = bf16[64,1024]{1,0:T(8,128)(2,1)} custom-call(bf16[64,1024]{1,0:T(8,128)(2,1)S(1)} %copy-done.7, bf16[32,2,96,128]{3,2,1,0:T(8,128)(2,1)S(1)} %bitcast.11, f32[64,3072]{1,0:T(8,128)S(1)} %get-tuple-element.5.bias_ref, f32[512,128]{1,0:T(8,128)S(1)} %get-tuple-element.6.attended_ref, f32[64,8]{1,0:T(8,128)S(1)} %get-tuple-element.7.level_ref), custom_call_target="tpu_custom_call" | custom-call | flops 1207959552 | bytes 2097152 | tf_op jit(solution)/shard_map/landing_decode/pallas_call | solution.py:386
  (13 shorter events, 0.0 us)
Async XLA Ops:
  0.6 13.7 %copy-start.11 = (s32[64]{0:T(128)S(1)}, s32[64]{0:T(128)}, u32[]{:S(2)}) copy-start(s32[64]{0:T(128)} %param.22) | copy-start | bytes 772
  0.6 13.8 %copy-start.3 = (bf16[1024,256]{1,0:T(8,128)(2,1)S(1)}, bf16[1024,256]{1,0:T(8,128)(2,1)}, u32[]{:S(2)}) copy-start(bf16[1024,256]{1,0:T(8,128)(2,1)} %weight_ref.1) | copy-start | bytes 1572868
  0.7 13.8 %copy-start.4 = (bf16[64,1024]{1,0:T(8,128)(2,1)S(1)}, bf16[64,1024]{1,0:T(8,128)(2,1)}, u32[]{:S(2)}) copy-start(bf16[64,1024]{1,0:T(8,128)(2,1)} %input_ref.1) | copy-start | bytes 393220
  0.7 21.5 %copy-start = (bf16[32,48,2,128]{3,2,1,0:T(2,128)(2,1)S(1)}, bf16[32,48,2,128]{3,2,1,0:T(2,128)(2,1)}, u32[]{:S(2)}) copy-start(bf16[32,48,2,128]{3,2,1,0:T(2,128)(2,1)} %param.16) | copy-start | bytes 2359300
  0.7 21.5 %copy-start.5 = (s32[32]{0:T(128)S(1)}, s32[32]{0:T(128)}, u32[]{:S(2)}) copy-start(s32[32]{0:T(128)} %pos_ref.1) | copy-start | bytes 388
  2.8 50.9 %all-to-all-start = ((bf16[32,192,128]{2,1,0:T(8,128)(2,1)}), bf16[32,192,128]{2,1,0:T(8,128)(2,1)S(1)}, u32[]{:S(2)}, u32[]{:S(2)}) async-start(bf16[32,192,128]{2,1,0:T(8,128)(2,1)} %bitcast.14), calls=%async_computation | async-start | bytes 3145728 | tf_op jit(solution)/shard_map/all_to_all | solution.py:426
  14.8 1.3 %collective-permute-start = (f32[64,128]{1,0:T(8,128)S(1)}, f32[64,128]{1,0:T(8,128)S(1)}, u32[]{:S(2)}, u32[]{:S(2)}) collective-permute-start(f32[64,128]{1,0:T(8,128)S(1)} %adapter_down.1), channel_id=1, source_target_pairs={{0,1},{1,0},{2,3},{3,2},{4,5},{5,4},{6,7},{7,6},{8,9},{9,8},{10,11... | collective-permute-start | bytes 98312 | tf_op jit(solution)/shard_map/ppermute | solution.py:222
  16.1 3.9 %collective-permute-start.1 = (f32[64,128]{1,0:T(8,128)S(1)}, f32[64,128]{1,0:T(8,128)S(1)}, u32[]{:S(2)}, u32[]{:S(2)}) collective-permute-start(f32[64,128]{1,0:T(8,128)S(1)} %add.9), channel_id=1, source_target_pairs={{0,2},{1,3},{2,0},{3,1},{4,6},{5,7},{6,4},{7,5},{8,10},{9,11},{10,... | collective-permute-start | bytes 98312 | tf_op jit(solution)/shard_map/ppermute | solution.py:222
  20.0 12.8 %collective-permute-start.2 = (f32[64,128]{1,0:T(8,128)S(1)}, f32[64,128]{1,0:T(8,128)S(1)}, u32[]{:S(2)}, u32[]{:S(2)}) collective-permute-start(f32[64,128]{1,0:T(8,128)S(1)} %add.10), channel_id=1, source_target_pairs={{0,4},{1,5},{2,6},{3,7},{4,0},{5,1},{6,2},{7,3},{8,12},{9,13},{10,... | collective-permute-start | bytes 98312 | tf_op jit(solution)/shard_map/ppermute | solution.py:222
  22.2 1.9 %copy-start.1 = (bf16[1536,1024]{1,0:T(8,128)(2,1)S(1)}, bf16[1536,1024]{1,0:T(8,128)(2,1)}, u32[]{:S(2)}) copy-start(bf16[1536,1024]{1,0:T(8,128)(2,1)} %query_ref.3) | copy-start | bytes 9437188
  24.1 1.9 %copy-start.2 = (bf16[32,192,2,128]{3,2,1,0:T(2,128)(2,1)S(1)}, bf16[32,192,2,128]{3,2,1,0:T(2,128)(2,1)}, u32[]{:S(2)}) copy-start(bf16[32,192,2,128]{3,2,1,0:T(2,128)(2,1)} %param.15) | copy-start | bytes 9437188
  25.9 6.7 %copy-start.10 = (s32[64,15]{0,1:T(8,128)S(1)}, s32[64,15]{0,1:T(8,128)}, u32[]{:S(2)}) copy-start(s32[64,15]{0,1:T(8,128)} %param.26) | copy-start | bytes 11524
  25.9 6.8 %copy-start.12 = (s32[64]{0:T(128)S(1)}, s32[64]{0:T(128)}, u32[]{:S(2)}) copy-start(s32[64]{0:T(128)} %param.27) | copy-start | bytes 772
  26.0 6.9 %copy-start.7 = (bf16[64,1024]{1,0:T(8,128)(2,1)S(1)}, bf16[64,1024]{1,0:T(8,128)(2,1)}, u32[]{:S(2)}) copy-start(bf16[64,1024]{1,0:T(8,128)(2,1)} %query_ref.5) | copy-start | bytes 393220
  26.0 6.9 %copy-start.8 = (bf16[256,128]{1,0:T(8,128)(2,1)S(1)}, bf16[256,128]{1,0:T(8,128)(2,1)}, u32[]{:S(2)}) copy-start(bf16[256,128]{1,0:T(8,128)(2,1)} %up_ref.1) | copy-start | bytes 196612
  26.0 6.9 %copy-start.9 = (bf16[64,2,128]{2,1,0:T(2,128)(2,1)S(1)}, bf16[64,2,128]{2,1,0:T(2,128)(2,1)}, u32[]{:S(2)}) copy-start(bf16[64,2,128]{2,1,0:T(2,128)(2,1)} %param.21) | copy-start | bytes 98308
  32.9 1.1 %copy-start.6 = (bf16[96,16,2,128]{3,2,1,0:T(2,128)(2,1)S(1)}, bf16[96,16,2,128]{3,2,1,0:T(2,128)(2,1)}, u32[]{:S(2)}) copy-start(bf16[96,16,2,128]{3,2,1,0:T(2,128)(2,1)} %param.25) | copy-start | bytes 2359300

commit v3 on v2

--- a/solution.py
+++ b/solution.py
@@ -18,7 +18,7 @@
 VMEM_BYTES = 24 * 1024 * 1024
 PACK_BYTES = 56 * 1024 * 1024
 PROMPT_BLOCK = 8
-HEAD_BLOCK = 4
+HEAD_BLOCK = 2
 LANDING_TOKENS = 768
 SAFE_TOTAL = 2.0**100
 
@@ -331,7 +331,7 @@
     )(query, pool, table, length, adapter, middle, up, base)
 
 
-def landing_kernel(query_ref, landing_ref, bias_ref, attended_ref, level_ref, out_ref):
+def landing_kernel(query_ref, landing_ref, bias_ref, attended_ref, level_ref, out_hbm, out_ref, out_sem):
     rows = query_ref.shape[0]
     heads = query_ref.shape[1] // HEAD_SIZE
     groups, cap, slot_rows, _ = landing_ref.shape
@@ -357,6 +357,12 @@
         for h in range(HEAD_BLOCK):
             lanes = slice((first + h) * HEAD_SIZE, (first + h + 1) * HEAD_SIZE)
             out_ref[:, lanes] = result[h * rows : (h + 1) * rows]
+
+    def leave(first):
+        lanes = pl.ds(first * HEAD_SIZE, HEAD_BLOCK * HEAD_SIZE)
+        return pltpu.make_async_copy(
+            out_ref.at[:, lanes], out_hbm.at[:, lanes], out_sem.at[first // HEAD_BLOCK]
+        )
 
     worst = jnp.zeros((8, HEAD_SIZE), jnp.float32)
     for first in range(0, heads, HEAD_BLOCK):
@@ -369,7 +375,11 @@
             weights = jnp.exp2(scores).astype(jnp.bfloat16).reshape(HEAD_BLOCK * rows, tokens)
             total = total + jnp.dot(weights, value, preferred_element_type=jnp.float32)
         finish(first, total)
+        leave(first).start()
         worst = jnp.maximum(worst, jnp.max(total[:, HEAD_SIZE:].reshape(-1, 8, HEAD_SIZE), axis=0))
+
+    for first in range(0, heads, HEAD_BLOCK):
+        leave(first).wait()
 
     @pl.when(jnp.logical_not(jnp.max(worst) < SAFE_TOTAL))
     def _():
@@ -378,6 +388,8 @@
             for c in range(groups // span):
                 top, total = attend(query, *part(c), top, total)
             finish(first, total)
+            leave(first).start()
+            leave(first).wait()
 
 
 def landing_decode(query, landing, bias, attended, level):
@@ -387,7 +399,11 @@
         landing_kernel,
         out_shape=jax.ShapeDtypeStruct(query.shape, jnp.bfloat16),
         in_specs=[in_vmem()] * 5,
-        out_specs=in_vmem(),
+        out_specs=pl.BlockSpec(memory_space=pl.ANY),
+        scratch_shapes=[
+            pltpu.VMEM(query.shape, query.dtype),
+            pltpu.SemaphoreType.DMA((query.shape[1] // (HEAD_BLOCK * HEAD_SIZE),)),
+        ],
         compiler_params=params(),
         cost_estimate=cost(
             stacked * tokens * HEAD_SIZE * 6, landing.size * 2 + stacked * 1024, stacked * tokens

time: 56.9 us -> 57 us (level)
  no operation moved by 1% of the time
where the time goes in v3:
time: 57 us; the launch traced here: 56.6 us
  waiting for transfers between devices  20.5 us (36%)
  Pallas kernels  15.8 us (28%)
  starting transfers between devices  14.2 us (25%)
  local copies, waits for them, and re-layouts  5.23 us (9%)
  between operations  0.94 us (2%)
    all_to_all x1, waiting for transfers between devices, body(): lax.all_to_all(outgoing.reshape(groups, -1, HEAD_SIZE), 'group', 0, 0, ti...  15.9 us
    all_to_all x1, starting transfers between devices, body(): lax.all_to_all(outgoing.reshape(groups, -1, HEAD_SIZE), 'group', 0, 0, ti...  11.5 us
    pallas_call x1, Pallas kernels, prefill(): pl.pallas_call(prefill_kernel, grid=(prompts // block,), out_shape=jax.Sh...  6.65 us
    unnamed x27, local copies, waits for them, and re-layouts  5.04 us
    ppermute x3, waiting for transfers between devices, sum_over_tensor(): x = x + lax.ppermute(x, 'tensor', [(i, i ^ stride) for i in range(count)])  4.58 us
    pallas_call x1, Pallas kernels, pool_decode(): pl.pallas_call(pool_kernel, out_shape=(jax.ShapeDtypeStruct((stacked, HEA...  3.8 us
    pallas_call x1, Pallas kernels, landing_decode(): pl.pallas_call(landing_kernel, out_shape=jax.ShapeDtypeStruct(query.shape...  2.8 us
    ppermute x3, starting transfers between devices, sum_over_tensor(): x = x + lax.ppermute(x, 'tensor', [(i, i ^ stride) for i in range(count)])  2.75 us
  transfers between devices with their start and end apart: 4, of which 3 were waited for; matrix products, arithmetic and copies ran while one was open for 1% of the time, Pallas kernels for 19%

profile of v3, /device:TPU:2, one launch (start us, length us, event | category | flops | bytes accessed | tf_op | source)
XLA Modules:
  0.0 56.6 jit_solution(3375941901041026967)
XLA Ops:
  0.6 0.0 copy-start.11
  0.6 0.0 copy-start.3
  0.7 0.0 copy-start.4
  0.7 0.0 copy-start
  0.7 0.0 copy-start.5
  0.7 2.2 %pack.1 = bf16[32,2,96,128]{3,2,1,0:T(8,128)(2,1)} custom-call(s32[32]{0:T(128)} %owner_hbm.1, bf16[32,96,128]{2,1,0:T(8,128)(2,1)} %bitcast.8), custom_call_target="tpu_custom_call" | custom-call | bytes 2359296 | tf_op jit(solution)/shard_map/pack/pallas_call | solution.py:101
  2.9 11.5 %all-to-all-start = ((bf16[32,192,128]{2,1,0:T(8,128)(2,1)}), bf16[32,192,128]{2,1,0:T(8,128)(2,1)S(1)}, u32[]{:S(2)}, u32[]{:S(2)}) async-start(bf16[32,192,128]{2,1,0:T(8,128)(2,1)} %bitcast.14), calls=%async_computation | async-start | bytes 3145728 | tf_op jit(solution)/shard_map/all_to_all | solution.py:442
  14.4 0.0 copy-done.11
  14.4 0.1 copy.19.adapter_ref
  14.5 0.3 adapter_down.1
  14.8 0.1 collective-permute-start
  14.9 1.2 %collective-permute-done = f32[64,128]{1,0:T(8,128)S(1)} collective-permute-done((f32[64,128]{1,0:T(8,128)S(1)}, f32[64,128]{1,0:T(8,128)S(1)}, u32[]{:S(2)}, u32[]{:S(2)}) %collective-permute-start) | collective-permute-done | bytes 32800 | tf_op jit(solution)/shard_map/ppermute | solution.py:222
  16.1 0.5 collective-permute-start.1
  16.7 3.4 %collective-permute-done.1 = f32[64,128]{1,0:T(8,128)S(1)} collective-permute-done((f32[64,128]{1,0:T(8,128)S(1)}, f32[64,128]{1,0:T(8,128)S(1)}, u32[]{:S(2)}, u32[]{:S(2)}) %collective-permute-start.1) | collective-permute-done | bytes 32800 | tf_op jit(solution)/shard_map/ppermute | solution.py:222
  20.0 2.1 %collective-permute-start.2 = (f32[64,128]{1,0:T(8,128)S(1)}, f32[64,128]{1,0:T(8,128)S(1)}, u32[]{:S(2)}, u32[]{:S(2)}) collective-permute-start(f32[64,128]{1,0:T(8,128)S(1)} %add.10), channel_id=1, source_target_pairs={{0,4},{1,5},{2,6},{3,7},{4,0},{5,1},{6,2},{7,3},{8,12},{9,13},{10,... | collective-permute-start | bytes 98312 | tf_op jit(solution)/shard_map/ppermute | solution.py:222
  22.2 0.0 copy-done
  22.2 1.9 %copy-done.1 = bf16[1536,1024]{1,0:T(8,128)(2,1)S(1)} copy-done((bf16[1536,1024]{1,0:T(8,128)(2,1)S(1)}, bf16[1536,1024]{1,0:T(8,128)(2,1)}, u32[]{:S(2)}) %copy-start.1) | copy-done | bytes 3145752
  24.1 1.9 %copy-done.2 = bf16[32,192,2,128]{3,2,1,0:T(2,128)(2,1)S(1)} copy-done((bf16[32,192,2,128]{3,2,1,0:T(2,128)(2,1)S(1)}, bf16[32,192,2,128]{3,2,1,0:T(2,128)(2,1)}, u32[]{:S(2)}) %copy-start.2) | copy-done | bytes 3145752
  26.0 0.0 copy-start.9
  26.0 6.6 %prefill.1 = bf16[1536,1024]{1,0:T(8,128)(2,1)} custom-call(s32[32]{0:T(128)S(1)} %copy-done.5, bf16[1536,1024]{1,0:T(8,128)(2,1)S(1)} %copy-done.1, bf16[32,384,128]{2,1,0:T(8,128)(2,1)S(1)} %bitcast.10, bf16[32,96,128]{2,1,0:T(8,128)(2,1)S(1)} %bitcast.9), custom_call_target="tpu_custom_call" | custom-call | flops 2415919104 | bytes 10223616 | tf_op jit(solution)/shard_map/prefill/pallas_call | solution.py:171
  32.6 0.0 copy-done.10
  32.6 0.1 copy.17.table_ref
  32.7 0.1 copy.18.length_ref
  32.8 0.0 collective-permute-done.2
  32.8 0.0 copy-done.7
  32.8 0.0 copy-done.8
  32.9 0.0 copy-done.9
  32.9 0.0 copy-start.6
  32.9 1.1 %copy-done.6 = bf16[96,16,2,128]{3,2,1,0:T(2,128)(2,1)S(1)} copy-done((bf16[96,16,2,128]{3,2,1,0:T(2,128)(2,1)S(1)}, bf16[96,16,2,128]{3,2,1,0:T(2,128)(2,1)}, u32[]{:S(2)}) %copy-start.6) | copy-done | bytes 786456
  34.0 3.8 %pool_decode.1 = (f32[512,128]{1,0:T(8,128)S(1)}, f32[64,8]{1,0:T(8,128)S(1)}, f32[64,3072]{1,0:T(8,128)S(1)}) custom-call(bf16[64,1024]{1,0:T(8,128)(2,1)S(1)} %copy-done.7, bf16[3072,128]{1,0:T(8,128)(2,1)S(1)} %bitcast.12, s32[64,15]{1,0:T(8,128)S(1)} %copy.17.table_ref, s32[64,1]{1,0:T(8,128)S(1)} %copy.18.length_ref, s32[64,1]{1,0:T(8,128)S(1)} %copy.19.adapter_ref, ...), custom_call_target="tpu_custom_call" | custom-call | flops 603979776 | bytes 1572864 | tf_op jit(solution)/shard_map/pool_decode/pallas_call | solution.py:312
  37.8 15.9 %all-to-all-done = bf16[32,192,128]{2,1,0:T(8,128)(2,1)S(1)} async-done(((bf16[32,192,128]{2,1,0:T(8,128)(2,1)}), bf16[32,192,128]{2,1,0:T(8,128)(2,1)S(1)}, u32[]{:S(2)}, u32[]{:S(2)}) %all-to-all-start) | async-done | bytes 1572896 | tf_op jit(solution)/shard_map/all_to_all | solution.py:442
  53.7 2.8 %landing_decode.1 = bf16[64,1024]{1,0:T(8,128)(2,1)} custom-call(bf16[64,1024]{1,0:T(8,128)(2,1)S(1)} %copy-done.7, bf16[32,2,96,128]{3,2,1,0:T(8,128)(2,1)S(1)} %bitcast.11, f32[64,3072]{1,0:T(8,128)S(1)} %get-tuple-element.5.bias_ref, f32[512,128]{1,0:T(8,128)S(1)} %get-tuple-element.6.attended_ref, f32[64,8]{1,0:T(8,128)S(1)} %get-tuple-element.7.level_ref), custom_call_target="tpu_custom_call" | custom-call | flops 1207959552 | bytes 2097152 | tf_op jit(solution)/shard_map/landing_decode/pallas_call | solution.py:398
  (13 shorter events, 0.0 us)
Async XLA Ops:
  0.6 13.7 %copy-start.11 = (s32[64]{0:T(128)S(1)}, s32[64]{0:T(128)}, u32[]{:S(2)}) copy-start(s32[64]{0:T(128)} %param.22) | copy-start | bytes 772
  0.6 13.8 %copy-start.3 = (bf16[1024,256]{1,0:T(8,128)(2,1)S(1)}, bf16[1024,256]{1,0:T(8,128)(2,1)}, u32[]{:S(2)}) copy-start(bf16[1024,256]{1,0:T(8,128)(2,1)} %weight_ref.1) | copy-start | bytes 1572868
  0.7 13.8 %copy-start.4 = (bf16[64,1024]{1,0:T(8,128)(2,1)S(1)}, bf16[64,1024]{1,0:T(8,128)(2,1)}, u32[]{:S(2)}) copy-start(bf16[64,1024]{1,0:T(8,128)(2,1)} %input_ref.1) | copy-start | bytes 393220
  0.7 21.5 %copy-start = (bf16[32,48,2,128]{3,2,1,0:T(2,128)(2,1)S(1)}, bf16[32,48,2,128]{3,2,1,0:T(2,128)(2,1)}, u32[]{:S(2)}) copy-start(bf16[32,48,2,128]{3,2,1,0:T(2,128)(2,1)} %param.16) | copy-start | bytes 2359300
  0.7 21.5 %copy-start.5 = (s32[32]{0:T(128)S(1)}, s32[32]{0:T(128)}, u32[]{:S(2)}) copy-start(s32[32]{0:T(128)} %pos_ref.1) | copy-start | bytes 388
  2.9 50.8 %all-to-all-start = ((bf16[32,192,128]{2,1,0:T(8,128)(2,1)}), bf16[32,192,128]{2,1,0:T(8,128)(2,1)S(1)}, u32[]{:S(2)}, u32[]{:S(2)}) async-start(bf16[32,192,128]{2,1,0:T(8,128)(2,1)} %bitcast.14), calls=%async_computation | async-start | bytes 3145728 | tf_op jit(solution)/shard_map/all_to_all | solution.py:442
  14.8 1.3 %collective-permute-start = (f32[64,128]{1,0:T(8,128)S(1)}, f32[64,128]{1,0:T(8,128)S(1)}, u32[]{:S(2)}, u32[]{:S(2)}) collective-permute-start(f32[64,128]{1,0:T(8,128)S(1)} %adapter_down.1), channel_id=1, source_target_pairs={{0,1},{1,0},{2,3},{3,2},{4,5},{5,4},{6,7},{7,6},{8,9},{9,8},{10,11... | collective-permute-start | bytes 98312 | tf_op jit(solution)/shard_map/ppermute | solution.py:222
  16.1 3.9 %collective-permute-start.1 = (f32[64,128]{1,0:T(8,128)S(1)}, f32[64,128]{1,0:T(8,128)S(1)}, u32[]{:S(2)}, u32[]{:S(2)}) collective-permute-start(f32[64,128]{1,0:T(8,128)S(1)} %add.9), channel_id=1, source_target_pairs={{0,2},{1,3},{2,0},{3,1},{4,6},{5,7},{6,4},{7,5},{8,10},{9,11},{10,... | collective-permute-start | bytes 98312 | tf_op jit(solution)/shard_map/ppermute | solution.py:222
  20.0 12.8 %collective-permute-start.2 = (f32[64,128]{1,0:T(8,128)S(1)}, f32[64,128]{1,0:T(8,128)S(1)}, u32[]{:S(2)}, u32[]{:S(2)}) collective-permute-start(f32[64,128]{1,0:T(8,128)S(1)} %add.10), channel_id=1, source_target_pairs={{0,4},{1,5},{2,6},{3,7},{4,0},{5,1},{6,2},{7,3},{8,12},{9,13},{10,... | collective-permute-start | bytes 98312 | tf_op jit(solution)/shard_map/ppermute | solution.py:222
  22.2 1.9 %copy-start.1 = (bf16[1536,1024]{1,0:T(8,128)(2,1)S(1)}, bf16[1536,1024]{1,0:T(8,128)(2,1)}, u32[]{:S(2)}) copy-start(bf16[1536,1024]{1,0:T(8,128)(2,1)} %query_ref.3) | copy-start | bytes 9437188
  24.1 1.9 %copy-start.2 = (bf16[32,192,2,128]{3,2,1,0:T(2,128)(2,1)S(1)}, bf16[32,192,2,128]{3,2,1,0:T(2,128)(2,1)}, u32[]{:S(2)}) copy-start(bf16[32,192,2,128]{3,2,1,0:T(2,128)(2,1)} %param.15) | copy-start | bytes 9437188
  26.0 6.7 %copy-start.10 = (s32[64,15]{0,1:T(8,128)S(1)}, s32[64,15]{0,1:T(8,128)}, u32[]{:S(2)}) copy-start(s32[64,15]{0,1:T(8,128)} %param.26) | copy-start | bytes 11524
  26.0 6.8 %copy-start.12 = (s32[64]{0:T(128)S(1)}, s32[64]{0:T(128)}, u32[]{:S(2)}) copy-start(s32[64]{0:T(128)} %param.27) | copy-start | bytes 772
  26.0 6.9 %copy-start.7 = (bf16[64,1024]{1,0:T(8,128)(2,1)S(1)}, bf16[64,1024]{1,0:T(8,128)(2,1)}, u32[]{:S(2)}) copy-start(bf16[64,1024]{1,0:T(8,128)(2,1)} %query_ref.5) | copy-start | bytes 393220
  26.0 6.9 %copy-start.8 = (bf16[256,128]{1,0:T(8,128)(2,1)S(1)}, bf16[256,128]{1,0:T(8,128)(2,1)}, u32[]{:S(2)}) copy-start(bf16[256,128]{1,0:T(8,128)(2,1)} %up_ref.1) | copy-start | bytes 196612
  26.0 6.9 %copy-start.9 = (bf16[64,2,128]{2,1,0:T(2,128)(2,1)S(1)}, bf16[64,2,128]{2,1,0:T(2,128)(2,1)}, u32[]{:S(2)}) copy-start(bf16[64,2,128]{2,1,0:T(2,128)(2,1)} %param.21) | copy-start | bytes 98308
  32.9 1.1 %copy-start.6 = (bf16[96,16,2,128]{3,2,1,0:T(2,128)(2,1)S(1)}, bf16[96,16,2,128]{3,2,1,0:T(2,128)(2,1)}, u32[]{:S(2)}) copy-start(bf16[96,16,2,128]{3,2,1,0:T(2,128)(2,1)} %param.25) | copy-start | bytes 2359300

commit v4 on v3

--- a/solution.py
+++ b/solution.py
@@ -97,7 +97,7 @@
 
 def pack(owner, stretch, groups):
     prompts, rows, _ = stretch.shape
-    parts = 4
+    parts = 8
     return pl.pallas_call(
         pack_kernel,
         out_shape=jax.ShapeDtypeStruct((groups, CAP, rows, HEAD_SIZE), jnp.bfloat16),

time: 57 us -> 57 us (level)
  no operation moved by 1% of the time
where the time goes in v4:
time: 57 us; the launch traced here: 56.7 us
  waiting for transfers between devices  20.5 us (36%)
  Pallas kernels  15.8 us (28%)
  starting transfers between devices  14.3 us (25%)
  local copies, waits for them, and re-layouts  5.23 us (9%)
  between operations  0.94 us (2%)
    all_to_all x1, waiting for transfers between devices, body(): lax.all_to_all(outgoing.reshape(groups, -1, HEAD_SIZE), 'group', 0, 0, ti...  15.9 us
    all_to_all x1, starting transfers between devices, body(): lax.all_to_all(outgoing.reshape(groups, -1, HEAD_SIZE), 'group', 0, 0, ti...  11.5 us
    pallas_call x1, Pallas kernels, prefill(): pl.pallas_call(prefill_kernel, grid=(prompts // block,), out_shape=jax.Sh...  6.65 us
    unnamed x27, local copies, waits for them, and re-layouts  5.04 us
    ppermute x3, waiting for transfers between devices, sum_over_tensor(): x = x + lax.ppermute(x, 'tensor', [(i, i ^ stride) for i in range(count)])  4.58 us
    pallas_call x1, Pallas kernels, pool_decode(): pl.pallas_call(pool_kernel, out_shape=(jax.ShapeDtypeStruct((stacked, HEA...  3.8 us
    pallas_call x1, Pallas kernels, landing_decode(): pl.pallas_call(landing_kernel, out_shape=jax.ShapeDtypeStruct(query.shape...  2.8 us
    ppermute x3, starting transfers between devices, sum_over_tensor(): x = x + lax.ppermute(x, 'tensor', [(i, i ^ stride) for i in range(count)])  2.75 us
  transfers between devices with their start and end apart: 4, of which 3 were waited for; matrix products, arithmetic and copies ran while one was open for 1% of the time, Pallas kernels for 19%

profile of v4, /device:TPU:2, one launch (start us, length us, event | category | flops | bytes accessed | tf_op | source)
XLA Modules:
  0.0 56.7 jit_solution(10685379616592023176)
XLA Ops:
  0.6 0.0 copy-start.11
  0.6 0.0 copy-start.3
  0.7 0.0 copy-start.4
  0.7 0.0 copy-start
  0.7 0.0 copy-start.5
  0.7 2.2 %pack.1 = bf16[32,2,96,128]{3,2,1,0:T(8,128)(2,1)} custom-call(s32[32]{0:T(128)} %owner_hbm.1, bf16[32,96,128]{2,1,0:T(8,128)(2,1)} %bitcast.8), custom_call_target="tpu_custom_call" | custom-call | bytes 2359296 | tf_op jit(solution)/shard_map/pack/pallas_call | solution.py:101
  2.9 11.5 %all-to-all-start = ((bf16[32,192,128]{2,1,0:T(8,128)(2,1)}), bf16[32,192,128]{2,1,0:T(8,128)(2,1)S(1)}, u32[]{:S(2)}, u32[]{:S(2)}) async-start(bf16[32,192,128]{2,1,0:T(8,128)(2,1)} %bitcast.14), calls=%async_computation | async-start | bytes 3145728 | tf_op jit(solution)/shard_map/all_to_all | solution.py:442
  14.4 0.0 copy-done.11
  14.4 0.1 copy.19.adapter_ref
  14.5 0.0 copy-done.3
  14.5 0.0 copy-done.4
  14.5 0.3 adapter_down.1
  14.9 0.1 collective-permute-start
  15.0 1.2 %collective-permute-done = f32[64,128]{1,0:T(8,128)S(1)} collective-permute-done((f32[64,128]{1,0:T(8,128)S(1)}, f32[64,128]{1,0:T(8,128)S(1)}, u32[]{:S(2)}, u32[]{:S(2)}) %collective-permute-start) | collective-permute-done | bytes 32800 | tf_op jit(solution)/shard_map/ppermute | solution.py:222
  16.2 0.5 collective-permute-start.1
  16.7 3.4 %collective-permute-done.1 = f32[64,128]{1,0:T(8,128)S(1)} collective-permute-done((f32[64,128]{1,0:T(8,128)S(1)}, f32[64,128]{1,0:T(8,128)S(1)}, u32[]{:S(2)}, u32[]{:S(2)}) %collective-permute-start.1) | collective-permute-done | bytes 32800 | tf_op jit(solution)/shard_map/ppermute | solution.py:222
  20.1 2.1 %collective-permute-start.2 = (f32[64,128]{1,0:T(8,128)S(1)}, f32[64,128]{1,0:T(8,128)S(1)}, u32[]{:S(2)}, u32[]{:S(2)}) collective-permute-start(f32[64,128]{1,0:T(8,128)S(1)} %add.10), channel_id=1, source_target_pairs={{0,4},{1,5},{2,6},{3,7},{4,0},{5,1},{6,2},{7,3},{8,12},{9,13},{10,... | collective-permute-start | bytes 98312 | tf_op jit(solution)/shard_map/ppermute | solution.py:222
  22.2 0.0 copy-done
  22.2 0.0 copy-done.5
  22.2 1.9 %copy-done.1 = bf16[1536,1024]{1,0:T(8,128)(2,1)S(1)} copy-done((bf16[1536,1024]{1,0:T(8,128)(2,1)S(1)}, bf16[1536,1024]{1,0:T(8,128)(2,1)}, u32[]{:S(2)}) %copy-start.1) | copy-done | bytes 3145752
  24.1 1.9 %copy-done.2 = bf16[32,192,2,128]{3,2,1,0:T(2,128)(2,1)S(1)} copy-done((bf16[32,192,2,128]{3,2,1,0:T(2,128)(2,1)S(1)}, bf16[32,192,2,128]{3,2,1,0:T(2,128)(2,1)}, u32[]{:S(2)}) %copy-start.2) | copy-done | bytes 3145752
  26.0 0.0 copy-start.9
  26.0 6.6 %prefill.1 = bf16[1536,1024]{1,0:T(8,128)(2,1)} custom-call(s32[32]{0:T(128)S(1)} %copy-done.5, bf16[1536,1024]{1,0:T(8,128)(2,1)S(1)} %copy-done.1, bf16[32,384,128]{2,1,0:T(8,128)(2,1)S(1)} %bitcast.10, bf16[32,96,128]{2,1,0:T(8,128)(2,1)S(1)} %bitcast.9), custom_call_target="tpu_custom_call" | custom-call | flops 2415919104 | bytes 10223616 | tf_op jit(solution)/shard_map/prefill/pallas_call | solution.py:171
  32.7 0.0 copy-done.10
  32.7 0.1 copy.17.table_ref
  32.8 0.1 copy.18.length_ref
  32.9 0.0 collective-permute-done.2
  32.9 0.0 copy-start.6
  32.9 1.1 %copy-done.6 = bf16[96,16,2,128]{3,2,1,0:T(2,128)(2,1)S(1)} copy-done((bf16[96,16,2,128]{3,2,1,0:T(2,128)(2,1)S(1)}, bf16[96,16,2,128]{3,2,1,0:T(2,128)(2,1)}, u32[]{:S(2)}) %copy-start.6) | copy-done | bytes 786456
  34.1 3.8 %pool_decode.1 = (f32[512,128]{1,0:T(8,128)S(1)}, f32[64,8]{1,0:T(8,128)S(1)}, f32[64,3072]{1,0:T(8,128)S(1)}) custom-call(bf16[64,1024]{1,0:T(8,128)(2,1)S(1)} %copy-done.7, bf16[3072,128]{1,0:T(8,128)(2,1)S(1)} %bitcast.12, s32[64,15]{1,0:T(8,128)S(1)} %copy.17.table_ref, s32[64,1]{1,0:T(8,128)S(1)} %copy.18.length_ref, s32[64,1]{1,0:T(8,128)S(1)} %copy.19.adapter_ref, ...), custom_call_target="tpu_custom_call" | custom-call | flops 603979776 | bytes 1572864 | tf_op jit(solution)/shard_map/pool_decode/pallas_call | solution.py:312
  37.9 15.9 %all-to-all-done = bf16[32,192,128]{2,1,0:T(8,128)(2,1)S(1)} async-done(((bf16[32,192,128]{2,1,0:T(8,128)(2,1)}), bf16[32,192,128]{2,1,0:T(8,128)(2,1)S(1)}, u32[]{:S(2)}, u32[]{:S(2)}) %all-to-all-start) | async-done | bytes 1572896 | tf_op jit(solution)/shard_map/all_to_all | solution.py:442
  53.7 2.8 %landing_decode.1 = bf16[64,1024]{1,0:T(8,128)(2,1)} custom-call(bf16[64,1024]{1,0:T(8,128)(2,1)S(1)} %copy-done.7, bf16[32,2,96,128]{3,2,1,0:T(8,128)(2,1)S(1)} %bitcast.11, f32[64,3072]{1,0:T(8,128)S(1)} %get-tuple-element.5.bias_ref, f32[512,128]{1,0:T(8,128)S(1)} %get-tuple-element.6.attended_ref, f32[64,8]{1,0:T(8,128)S(1)} %get-tuple-element.7.level_ref), custom_call_target="tpu_custom_call" | custom-call | flops 1207959552 | bytes 2097152 | tf_op jit(solution)/shard_map/landing_decode/pallas_call | solution.py:398
  (13 shorter events, 0.0 us)
Async XLA Ops:
  0.6 13.8 %copy-start.11 = (s32[64]{0:T(128)S(1)}, s32[64]{0:T(128)}, u32[]{:S(2)}) copy-start(s32[64]{0:T(128)} %param.22) | copy-start | bytes 772
  0.6 13.9 %copy-start.3 = (bf16[1024,256]{1,0:T(8,128)(2,1)S(1)}, bf16[1024,256]{1,0:T(8,128)(2,1)}, u32[]{:S(2)}) copy-start(bf16[1024,256]{1,0:T(8,128)(2,1)} %weight_ref.1) | copy-start | bytes 1572868
  0.7 13.9 %copy-start.4 = (bf16[64,1024]{1,0:T(8,128)(2,1)S(1)}, bf16[64,1024]{1,0:T(8,128)(2,1)}, u32[]{:S(2)}) copy-start(bf16[64,1024]{1,0:T(8,128)(2,1)} %input_ref.1) | copy-start | bytes 393220
  0.7 21.6 %copy-start = (bf16[32,48,2,128]{3,2,1,0:T(2,128)(2,1)S(1)}, bf16[32,48,2,128]{3,2,1,0:T(2,128)(2,1)}, u32[]{:S(2)}) copy-start(bf16[32,48,2,128]{3,2,1,0:T(2,128)(2,1)} %param.16) | copy-start | bytes 2359300
  0.7 21.6 %copy-start.5 = (s32[32]{0:T(128)S(1)}, s32[32]{0:T(128)}, u32[]{:S(2)}) copy-start(s32[32]{0:T(128)} %pos_ref.1) | copy-start | bytes 388
  2.9 50.9 %all-to-all-start = ((bf16[32,192,128]{2,1,0:T(8,128)(2,1)}), bf16[32,192,128]{2,1,0:T(8,128)(2,1)S(1)}, u32[]{:S(2)}, u32[]{:S(2)}) async-start(bf16[32,192,128]{2,1,0:T(8,128)(2,1)} %bitcast.14), calls=%async_computation | async-start | bytes 3145728 | tf_op jit(solution)/shard_map/all_to_all | solution.py:442
  14.9 1.3 %collective-permute-start = (f32[64,128]{1,0:T(8,128)S(1)}, f32[64,128]{1,0:T(8,128)S(1)}, u32[]{:S(2)}, u32[]{:S(2)}) collective-permute-start(f32[64,128]{1,0:T(8,128)S(1)} %adapter_down.1), channel_id=1, source_target_pairs={{0,1},{1,0},{2,3},{3,2},{4,5},{5,4},{6,7},{7,6},{8,9},{9,8},{10,11... | collective-permute-start | bytes 98312 | tf_op jit(solution)/shard_map/ppermute | solution.py:222
  16.2 3.9 %collective-permute-start.1 = (f32[64,128]{1,0:T(8,128)S(1)}, f32[64,128]{1,0:T(8,128)S(1)}, u32[]{:S(2)}, u32[]{:S(2)}) collective-permute-start(f32[64,128]{1,0:T(8,128)S(1)} %add.9), channel_id=1, source_target_pairs={{0,2},{1,3},{2,0},{3,1},{4,6},{5,7},{6,4},{7,5},{8,10},{9,11},{10,... | collective-permute-start | bytes 98312 | tf_op jit(solution)/shard_map/ppermute | solution.py:222
  20.1 12.8 %collective-permute-start.2 = (f32[64,128]{1,0:T(8,128)S(1)}, f32[64,128]{1,0:T(8,128)S(1)}, u32[]{:S(2)}, u32[]{:S(2)}) collective-permute-start(f32[64,128]{1,0:T(8,128)S(1)} %add.10), channel_id=1, source_target_pairs={{0,4},{1,5},{2,6},{3,7},{4,0},{5,1},{6,2},{7,3},{8,12},{9,13},{10,... | collective-permute-start | bytes 98312 | tf_op jit(solution)/shard_map/ppermute | solution.py:222
  22.2 1.9 %copy-start.1 = (bf16[1536,1024]{1,0:T(8,128)(2,1)S(1)}, bf16[1536,1024]{1,0:T(8,128)(2,1)}, u32[]{:S(2)}) copy-start(bf16[1536,1024]{1,0:T(8,128)(2,1)} %query_ref.3) | copy-start | bytes 9437188
  24.1 1.9 %copy-start.2 = (bf16[32,192,2,128]{3,2,1,0:T(2,128)(2,1)S(1)}, bf16[32,192,2,128]{3,2,1,0:T(2,128)(2,1)}, u32[]{:S(2)}) copy-start(bf16[32,192,2,128]{3,2,1,0:T(2,128)(2,1)} %param.15) | copy-start | bytes 9437188
  26.0 6.7 %copy-start.10 = (s32[64,15]{0,1:T(8,128)S(1)}, s32[64,15]{0,1:T(8,128)}, u32[]{:S(2)}) copy-start(s32[64,15]{0,1:T(8,128)} %param.26) | copy-start | bytes 11524
  26.0 6.8 %copy-start.12 = (s32[64]{0:T(128)S(1)}, s32[64]{0:T(128)}, u32[]{:S(2)}) copy-start(s32[64]{0:T(128)} %param.27) | copy-start | bytes 772
  26.0 6.9 %copy-start.7 = (bf16[64,1024]{1,0:T(8,128)(2,1)S(1)}, bf16[64,1024]{1,0:T(8,128)(2,1)}, u32[]{:S(2)}) copy-start(bf16[64,1024]{1,0:T(8,128)(2,1)} %query_ref.5) | copy-start | bytes 393220
  26.0 6.9 %copy-start.8 = (bf16[256,128]{1,0:T(8,128)(2,1)S(1)}, bf16[256,128]{1,0:T(8,128)(2,1)}, u32[]{:S(2)}) copy-start(bf16[256,128]{1,0:T(8,128)(2,1)} %up_ref.1) | copy-start | bytes 196612
  26.0 6.9 %copy-start.9 = (bf16[64,2,128]{2,1,0:T(2,128)(2,1)S(1)}, bf16[64,2,128]{2,1,0:T(2,128)(2,1)}, u32[]{:S(2)}) copy-start(bf16[64,2,128]{2,1,0:T(2,128)(2,1)} %param.21) | copy-start | bytes 98308
  32.9 1.1 %copy-start.6 = (bf16[96,16,2,128]{3,2,1,0:T(2,128)(2,1)S(1)}, bf16[96,16,2,128]{3,2,1,0:T(2,128)(2,1)}, u32[]{:S(2)}) copy-start(bf16[96,16,2,128]{3,2,1,0:T(2,128)(2,1)} %param.25) | copy-start | bytes 2359300
